TPU v7x, 32 devices: a whole 2x2x4 slice. The times are simulated.
32 devices in a mesh: pb: 2 (over x), ka: 4 (over y, core), ha: 4 (over z).
Axes of the slice: x: 2, y: 2, z: 4, core: 2. Of those that a mesh axis runs over, the one named last changes fastest.
Arguments:
- queries: bfloat16 [1024, 64, 128], P(('pb', 'ka'), 'ha'), may hold values from -8 to 8
- keys: bfloat16 [1024, 8, 128], P(('pb', 'ka'), 'ha'), may hold values from -4.5 to 4.5
- values: bfloat16 [1024, 8, 128], P(('pb', 'ka'), 'ha'), may hold values from -12 to 12
- out_grad: bfloat16 [1024, 64, 128], P(('pb', 'ka'), 'ha'), may hold values from -6 to 6
Outputs:
- attended: bfloat16 [1024, 64, 128], P(('pb', 'ka'), 'ha')
- query_grad: bfloat16 [1024, 64, 128], P(('pb', 'ka'), 'ha')
- key_grad: bfloat16 [1024, 8, 128], P(('pb', 'ka'), 'ha')
- value_grad: bfloat16 [1024, 8, 128], P(('pb', 'ka'), 'ha')
All inputs are finite; a program needn't handle non-finite values.
Results may differ from a plain program's by a relative error of at most 0.0097.
Values may be sent and summed in bfloat16 or wider, within the bound.
A program may use at most 128 MiB of HBM per device.

v0:
```python
import math

import jax
import jax.numpy as jnp
from jax import lax
from jax.sharding import PartitionSpec as P

HEAD_DIM = 128
GROUP = 8


def make_absorb(grouped, scaling):

    def absorb(running, pieces, first_row):
        run_max, run_total, run_sum = running
        key_piece, value_piece = pieces
        scores = (
            jnp.einsum("qhgd,khd->hgqk", grouped, key_piece, preferred_element_type=jnp.float32)
            * scaling
        )
        new_max = jnp.maximum(run_max, jnp.max(scores, axis=-1))
        factor = jnp.exp(run_max - new_max)
        weights = jnp.exp(scores - new_max[..., None])
        run_total = run_total * factor + jnp.sum(weights, axis=-1)
        run_sum = run_sum * factor[..., None] + jnp.einsum(
            "hgqk,khd->hgqd",
            weights,
            value_piece.astype(jnp.float32),
            preferred_element_type=jnp.float32,
            precision=lax.Precision.HIGHEST,
        )
        return (new_max, run_total, run_sum)

    return absorb


def start_stats(kv_count, query_total):
    stat_shape = (kv_count, GROUP, query_total)
    return (
        jnp.full(stat_shape, -jnp.inf, jnp.float32),
        jnp.zeros(stat_shape, jnp.float32),
        jnp.zeros(stat_shape + (HEAD_DIM,), jnp.float32),
    )


def backward_blocks(query_heads, grad_heads, log_total, row_dots, key_rows, value_rows, scaling):
    key_total = key_rows.shape[0]
    block_width = math.gcd(key_total, 512)

    def visit_block(grad_running, position):
        first_row = position * block_width
        key_block = lax.dynamic_slice_in_dim(key_rows, first_row, block_width, 0)
        value_block = lax.dynamic_slice_in_dim(value_rows, first_row, block_width, 0)
        scores = (
            jnp.einsum("qhgd,khd->hgqk", query_heads, key_block, preferred_element_type=jnp.float32)
            * scaling
        )
        probs = jnp.exp(scores - log_total[..., None])
        value_part = jnp.einsum(
            "hgqk,qhgd->khd",
            probs.astype(jnp.bfloat16),
            grad_heads,
            preferred_element_type=jnp.float32,
        )
        grad_probs = jnp.einsum(
            "qhgd,khd->hgqk", grad_heads, value_block, preferred_element_type=jnp.float32
        )
        grad_scores = (scaling * probs * (grad_probs - row_dots[..., None])).astype(jnp.bfloat16)
        grad_running = grad_running + jnp.einsum(
            "hgqk,khd->qhgd", grad_scores, key_block, preferred_element_type=jnp.float32
        )
        key_part = jnp.einsum(
            "hgqk,qhgd->khd", grad_scores, query_heads, preferred_element_type=jnp.float32
        )
        return (grad_running, (key_part, value_part))

    initial = jnp.zeros(query_heads.shape, jnp.float32)
    block_count = key_total // block_width
    grad_query, (key_parts, value_parts) = lax.scan(
        visit_block, initial, jnp.arange(block_count, dtype=jnp.int32)
    )
    tail_shape = key_rows.shape
    return (grad_query, key_parts.reshape(tail_shape), value_parts.reshape(tail_shape))


def on_device(queries, keys, values, out_grad):
    local_rows = queries.shape[0]
    head_count = queries.shape[1]
    kv_count = keys.shape[1]
    scaling = HEAD_DIM ** (-0.5)
    own_queries = queries.reshape(local_rows, kv_count, GROUP, HEAD_DIM)
    every_key, every_value = (
        lax.all_gather(keys, ("pb", "ka"), axis=0, tiled=True),
        lax.all_gather(values, ("pb", "ka"), axis=0, tiled=True),
    )
    key_total = every_key.shape[0]
    block_width = math.gcd(key_total, 512)
    absorb_own = make_absorb(own_queries, scaling)

    def visit_keys(running, position):
        first_row = position * block_width
        key_block = lax.dynamic_slice_in_dim(every_key, first_row, block_width, 0)
        value_block = lax.dynamic_slice_in_dim(every_value, first_row, block_width, 0)
        return (absorb_own(running, (key_block, value_block), first_row), None)

    (own_max, own_total, own_sum), unused = lax.scan(
        visit_keys,
        start_stats(kv_count, local_rows),
        jnp.arange(key_total // block_width, dtype=jnp.int32),
    )
    exact_out = own_sum / own_total[..., None]
    output_heads = exact_out.astype(jnp.bfloat16)
    log_total = own_max + jnp.log(own_total)
    attended = jnp.transpose(output_heads, (2, 0, 1, 3)).reshape(local_rows, head_count, HEAD_DIM)
    grad_heads = out_grad.reshape(local_rows, kv_count, GROUP, HEAD_DIM)
    row_dots = jnp.einsum(
        "hgqd,qhgd->hgq",
        exact_out,
        grad_heads.astype(jnp.float32),
        preferred_element_type=jnp.float32,
    )
    wide_key, wide_value = (every_key, every_value)
    grad_query, key_terms, value_terms = backward_blocks(
        own_queries, grad_heads, log_total, row_dots, wide_key, wide_value, scaling
    )
    grad_key, grad_value = (
        lax.psum_scatter(key_terms, ("pb", "ka"), scatter_dimension=0, tiled=True),
        lax.psum_scatter(value_terms, ("pb", "ka"), scatter_dimension=0, tiled=True),
    )
    query_grad = grad_query.astype(jnp.bfloat16).reshape(local_rows, head_count, HEAD_DIM)
    return (attended, query_grad, grad_key.astype(jnp.bfloat16), grad_value.astype(jnp.bfloat16))


def solution(mesh):
    return jax.shard_map(
        on_device,
        mesh=mesh,
        in_specs=(
            P(("pb", "ka"), "ha", None),
            P(("pb", "ka"), "ha", None),
            P(("pb", "ka"), "ha", None),
            P(("pb", "ka"), "ha", None),
        ),
        out_specs=(
            P(("pb", "ka"), "ha", None),
            P(("pb", "ka"), "ha", None),
            P(("pb", "ka"), "ha", None),
            P(("pb", "ka"), "ha", None),
        ),
        check_vma=False,
    )
```

profile of v0, /device:TPU:0, one launch (start us, length us, event | category | flops | bytes accessed | tf_op | source)
XLA Modules:
  0.0 118.1 jit_solution(14028876927215031146)
XLA Ops:
  0.6 1.2 %dynamic-slice = u32[1]{0:T(128)} dynamic-slice(u32[32]{0:T(128)} %constant.47, u32[]{:T(128)S(6)} %add.40), dynamic_slice_sizes={1} | dynamic-slice | bytes 12
  2.6 0.9 copy.22
  3.4 0.9 copy.24
  4.3 11.3 %all_gather.7 = bf16[1024,2,128]{2,0,1:T(8,128)(2,1)S(1)} all-gather(bf16[128,2,128]{2,0,1:T(8,128)(2,1)S(1)} %copy.24), channel_id=1, replica_groups=mesh['pb'=2,'ka'=4,'ha'=4] {'pb','ka'}, dimensions={0}, use_global_device_ids=true | all-gather | bytes 589824 | tf_op jit(solution)/shard_map/all_gather | solution.py:94
  15.6 9.8 %all_gather.6 = bf16[1024,2,128]{2,0,1:T(8,128)(2,1)S(1)} all-gather(bf16[128,2,128]{2,0,1:T(8,128)(2,1)S(1)} %copy.22), channel_id=1, replica_groups=mesh['pb'=2,'ka'=4,'ha'=4] {'pb','ka'}, dimensions={0}, use_global_device_ids=true | all-gather | bytes 589824 | tf_op jit(solution)/shard_map/all_gather | solution.py:93
  25.4 1.2 copy.23
  26.6 1.2 copy.26
  27.8 15.2 %while.30 = (s32[]{:T(128)}, f32[2,8,128]{2,1,0:T(8,128)S(1)}, f32[2,8,128]{2,1,0:T(8,128)S(1)}, f32[2,8,128,128]{3,2,1,0:T(8,128)}, s32[2]{0:T(128)S(1)}, /*ind...) while((s32[]{:T(128)}, f32[2,8,128]{2,1,0:T(8,128)S(1)}, ...), condition=%wide.region_3.4_spmd.clone, body=%wide.region_0.3_spmd.clone.sunk | while | flops 1887184896 | bytes 24248580 | solution.py:106
  27.8 0.6 dynamic_slice.56
  29.1 0.0 copy-start
  29.1 0.7 bitcast_reduce_fusion.2
  29.8 0.7 fusion.71
  30.5 0.0 copy-done
  30.6 3.9 %fusion.73 = f32[2,8,128,128]{3,2,1,0:T(8,128)S(1)} fusion(f32[2,512,128,8]{2,1,3,0:T(8,128)S(1)} %get-tuple-element.338, f32[2,8,128]{2,1,0:T(8,128)S(1)} %select_maximum_fusion.2, f32[2,8,128,128]{3,2,1,0:T(8,128)S(1)} %copy-done, f32[2,8,128]{2,1,0:T(8,128)S(1)} %get-tuple-element.340, pred[]{:T(512)S(6)} %compare.6, ...), kind=kOutput, calls=%fused_computation.7.clone.1 | convolution fusion | flops 1613496320 | bytes 6569989 | tf_op jit(solution)/shard_map/while/body/eval_jaxpr/hgqk,khd->hgqd/dot_general | solution.py:25
  34.4 0.0 copy-start.1
  34.4 1.0 copy-done.1
  35.4 0.6 dynamic_slice.56
  36.7 0.0 copy-start
  36.7 0.7 bitcast_reduce_fusion.2
  37.4 0.7 fusion.71
  38.1 0.0 copy-done
  38.1 3.9 %fusion.73 = f32[2,8,128,128]{3,2,1,0:T(8,128)S(1)} fusion(f32[2,512,128,8]{2,1,3,0:T(8,128)S(1)} %get-tuple-element.338, f32[2,8,128]{2,1,0:T(8,128)S(1)} %select_maximum_fusion.2, f32[2,8,128,128]{3,2,1,0:T(8,128)S(1)} %copy-done, f32[2,8,128]{2,1,0:T(8,128)S(1)} %get-tuple-element.340, pred[]{:T(512)S(6)} %compare.6, ...), kind=kOutput, calls=%fused_computation.7.clone.1 | convolution fusion | flops 1613496320 | bytes 6569989 | tf_op jit(solution)/shard_map/while/body/eval_jaxpr/hgqk,khd->hgqd/dot_general | solution.py:25
  42.0 0.0 copy-start.1
  42.0 1.0 copy-done.1
  43.0 2.5 %multiply_reduce_fusion = (f32[2,8,128]{2,1,0:T(8,128)S(1)}, bf16[128,2,8,128]{3,0,2,1:T(8,128)(2,1)}) fusion(bf16[2,8,128,128]{3,1,0,2:T(8,128)(2,1)} %bitcast.143, f32[2,8,128,128]{3,2,1,0:T(8,128)} %get-tuple-element.107, f32[2,8,128]{2,1,0:T(8,128)S(1)} %get-tuple-element.108), kind=kLoop, calls=%fused_computation.47 | loop fusion | flops 1308672 | bytes 2113536 | tf_op jit(solution)/shard_map/hgqd,qhgd->hgq/dot_general | solution.py:116
  45.5 15.7 %while.31 = (s32[]{:T(128)}, f32[128,2,8,128]{0,3,2,1:T(8,128)S(1)}, f32[2,512,2,128]{3,2,1,0:T(2,128)}, f32[2,512,2,128]{3,2,1,0:T(2,128)}, s32[2]{0:T(128)S(1)...) while((s32[]{:T(128)}, ...), condition=%wide.region_5.6_spmd.clone, body=%wide.region_4.5_spmd.clone.sunk | while | flops 1352138752 | bytes 43802968 | solution.py:79
  45.5 0.6 dynamic_slice.60
  46.8 0.7 fusion.84
  47.5 0.8 fusion.87
  48.3 1.3 %fusion.85 = bf16[2,8,128,512]{2,3,1,0:T(8,128)(2,1)S(1)} fusion(f32[2,512,128,8]{2,1,3,0:T(8,128)S(1)} %fusion.84, bf16[128,2,8,128]{3,0,2,1:T(8,128)(2,1)S(1)} %get-tuple-element.429, f32[2,8,128]{2,1,0:T(8,128)S(1)} %get-tuple-element.430, f32[2,8,128]{2,1,0:T(8,128)S(1)} %get-tuple-element.427, ...), kind=kOutput, calls=%fused_computation.23.clone.1 | convolution fusion | flops 274726912 | bytes 7094276 | tf_op jit(solution)/shard_map/while/body/eval_jaxpr/qhgd,khd->hgqk/dot_general | solution.py:65
  49.6 0.0 copy-start.2
  49.6 0.0 copy-start.5
  49.6 0.7 convolution_bitcast_fusion.3
  50.3 0.7 fusion.86
  51.0 0.0 copy-done.2
  51.0 0.1 copy-done.5
  51.1 0.9 copy_dynamic-update-slice_fusion.3
  52.0 0.0 copy-start.3
  52.0 0.0 copy-start.6
  52.0 1.0 copy-done.3
  53.0 0.3 copy-done.6
  53.4 0.6 dynamic_slice.60
  54.6 0.7 fusion.84
  55.3 0.8 fusion.87
  56.1 1.3 %fusion.85 = bf16[2,8,128,512]{2,3,1,0:T(8,128)(2,1)S(1)} fusion(f32[2,512,128,8]{2,1,3,0:T(8,128)S(1)} %fusion.84, bf16[128,2,8,128]{3,0,2,1:T(8,128)(2,1)S(1)} %get-tuple-element.429, f32[2,8,128]{2,1,0:T(8,128)S(1)} %get-tuple-element.430, f32[2,8,128]{2,1,0:T(8,128)S(1)} %get-tuple-element.427, ...), kind=kOutput, calls=%fused_computation.23.clone.1 | convolution fusion | flops 274726912 | bytes 7094276 | tf_op jit(solution)/shard_map/while/body/eval_jaxpr/qhgd,khd->hgqk/dot_general | solution.py:65
  57.4 0.0 copy-start.2
  57.4 0.0 copy-start.5
  57.4 0.7 convolution_bitcast_fusion.3
  58.2 0.7 fusion.86
  58.8 0.0 copy-done.2
  58.8 0.1 copy-done.5
  59.0 0.9 copy_dynamic-update-slice_fusion.3
  59.9 0.0 copy-start.3
  59.9 0.0 copy-start.6
  59.9 1.0 copy-done.3
  60.9 0.3 copy-done.6
  61.2 0.0 copy-start.4
  61.2 0.1 convert_element_type.21
  61.3 1.2 %copy.27 = bf16[128,2,8,128]{3,2,1,0:T(8,128)(2,1)} copy(bf16[128,2,8,128]{0,3,2,1:T(8,128)(2,1)S(1)} %convert_element_type.21) | data formatting | bytes 1048576 | tf_op jit(solution)/shard_map/convert_element_type | solution.py:130
  62.5 2.2 %copy.55 = bf16[128,2,8,128]{3,2,1,0:T(8,128)(2,1)} copy(bf16[128,2,8,128]{3,0,2,1:T(8,128)(2,1)} %get-tuple-element.223) | data formatting | bytes 1048576 | tf_op jit(solution)/shard_map/transpose | solution.py:114
  64.7 0.0 copy-done.4
  64.7 52.7 %all-reduce.4 = (bf16[1024,2,128]{2,1,0:T(2,128)(2,1)S(1)}, bf16[1024,2,128]{2,1,0:T(2,128)(2,1)S(1)}) all-reduce(f32[1024,2,128]{2,1,0:T(2,128)} %bitcast.145, f32[1024,2,128]{2,1,0:T(2,128)S(1)} %bitcast.144), channel_id=2, replica_groups=mesh['pb'=2,'ka'=4,'ha'=4] {'pb','ka'}, use_global_device_ids=true, to_apply=%region_6.7.clone | all-reduce | flops 524288 | bytes 3145728
  117.4 0.8 dynamic-slice_convert_fusion
  (15 shorter events, 0.1 us)
Async XLA Ops:
  29.1 1.5 %copy-start = (f32[2,8,128,128]{3,2,1,0:T(8,128)S(1)}, f32[2,8,128,128]{3,2,1,0:T(8,128)}, u32[]{:S(2)}) copy-start(f32[2,8,128,128]{3,2,1,0:T(8,128)} %get-tuple-element.369) | copy-start | bytes 3145732 | tf_op jit(solution)/shard_map/while
  34.4 1.0 copy-start.1
  36.7 1.5 %copy-start = (f32[2,8,128,128]{3,2,1,0:T(8,128)S(1)}, f32[2,8,128,128]{3,2,1,0:T(8,128)}, u32[]{:S(2)}) copy-start(f32[2,8,128,128]{3,2,1,0:T(8,128)} %get-tuple-element.369) | copy-start | bytes 3145732 | tf_op jit(solution)/shard_map/while
  42.0 1.0 copy-start.1
  49.6 1.4 %copy-start.2 = (f32[2,512,2,128]{3,2,1,0:T(2,128)S(1)}, f32[2,512,2,128]{3,2,1,0:T(2,128)}, u32[]{:S(2)}) copy-start(f32[2,512,2,128]{3,2,1,0:T(2,128)} %get-tuple-element.408) | copy-start | bytes 3145732 | tf_op jit(solution)/shard_map/while
  49.6 1.5 %copy-start.5 = (f32[2,512,2,128]{3,2,1,0:T(2,128)S(1)}, f32[2,512,2,128]{3,2,1,0:T(2,128)}, u32[]{:S(2)}) copy-start(f32[2,512,2,128]{3,2,1,0:T(2,128)} %get-tuple-element.407) | copy-start | bytes 3145732 | tf_op jit(solution)/shard_map/while
  52.0 1.0 copy-start.3
  52.0 1.3 %copy-start.6 = (f32[2,512,2,128]{3,2,1,0:T(2,128)}, f32[2,512,2,128]{3,2,1,0:T(2,128)S(1)}, u32[]{:S(2)}) copy-start(f32[2,512,2,128]{3,2,1,0:T(2,128)S(1)} %get-tuple-element.422) | copy-start | bytes 3145732 | tf_op jit(solution)/shard_map/while
  57.4 1.4 %copy-start.2 = (f32[2,512,2,128]{3,2,1,0:T(2,128)S(1)}, f32[2,512,2,128]{3,2,1,0:T(2,128)}, u32[]{:S(2)}) copy-start(f32[2,512,2,128]{3,2,1,0:T(2,128)} %get-tuple-element.408) | copy-start | bytes 3145732 | tf_op jit(solution)/shard_map/while
  57.4 1.5 %copy-start.5 = (f32[2,512,2,128]{3,2,1,0:T(2,128)S(1)}, f32[2,512,2,128]{3,2,1,0:T(2,128)}, u32[]{:S(2)}) copy-start(f32[2,512,2,128]{3,2,1,0:T(2,128)} %get-tuple-element.407) | copy-start | bytes 3145732 | tf_op jit(solution)/shard_map/while
  59.9 1.0 copy-start.3
  59.9 1.3 %copy-start.6 = (f32[2,512,2,128]{3,2,1,0:T(2,128)}, f32[2,512,2,128]{3,2,1,0:T(2,128)S(1)}, u32[]{:S(2)}) copy-start(f32[2,512,2,128]{3,2,1,0:T(2,128)S(1)} %get-tuple-element.422) | copy-start | bytes 3145732 | tf_op jit(solution)/shard_map/while
  61.2 3.5 %copy-start.4 = (f32[2,512,2,128]{3,2,1,0:T(2,128)S(1)}, f32[2,512,2,128]{3,2,1,0:T(2,128)}, u32[]{:S(2)}) copy-start(f32[2,512,2,128]{3,2,1,0:T(2,128)} %get-tuple-element.112) | copy-start | bytes 3145732
where the time goes:
time: 119 us; the launch traced here: 118 us
  blocking collectives  73.8 us (62%)
  local copies, waits for them, and re-layouts  18.4 us (15%)
  matrix products  17.5 us (15%)
  other arithmetic  4.05 us (3%)
  loops' own time  2.93 us (2%)
  between operations  1.38 us (1%)
    unnamed x1, blocking collectives  52.7 us
    all_gather x1, blocking collectives, on_device(): lax.all_gather(values, ('pb', 'ka'), axis=0, tiled=True)  11.3 us
    all_gather x1, blocking collectives, on_device(): lax.all_gather(keys, ('pb', 'ka'), axis=0, tiled=True)  9.82 us
    dot_general x2, matrix products, absorb(): jnp.einsum('hgqk,khd->hgqd', weights, value_piece.astype(jnp.float32), pr...  7.71 us
    unnamed x7, local copies, waits for them, and re-layouts  5.31 us
    while x26, local copies, waits for them, and re-layouts  4.89 us
    dot_general x2, matrix products, visit_block(): jnp.einsum('qhgd,khd->hgqk', grad_heads, value_block, preferred_element_t...  2.65 us
    dot_general x1, other arithmetic, on_device(): jnp.einsum('hgqd,qhgd->hgq', exact_out, grad_heads.astype(jnp.float32), p...  2.52 us

commit v1 on v0

v1 whole, which is shorter than its diff:
```python
import functools
import math

import jax
import jax.numpy as jnp
from jax import lax
from jax.experimental import pallas as pl
from jax.experimental.pallas import tpu as pltpu
from jax.sharding import PartitionSpec as P

MESH = pl.DeviceIdType.MESH
F32 = jnp.float32
HALF = jnp.bfloat16
NT = (((1,), (1,)), ((), ()))


def fold_rows(x, op):
    return op(x.reshape(x.shape[0] // 8, 8, x.shape[1]), axis=0)


def kernel(dims, k_ref, v_ref, q_ref, g_ref, out_ref, dq_ref, dk_ref, dv_ref,
           kv_stage, kv, kv_t, qg_stage, qg, scores, grad_probs, tops, inverse, dots,
           out_t, dq_t, back, parts, terms,
           kv_send, kv_recv, qg_send, qg_recv, term_send, term_recv, back_send, back_recv):
    pb_size, ka_size, split, group, width = dims
    rows = k_ref.shape[0]
    depth = k_ref.shape[2]
    scaling = depth ** (-0.5)
    exponent = scaling * math.log2(math.e)
    lines = ka_size // split
    units = pb_size * lines
    heavy = rows * group
    blocks = split * heavy // width
    half_blocks = heavy // width

    pb, ka, ha = lax.axis_index("pb"), lax.axis_index("ka"), lax.axis_index("ha")
    core = lax.rem(ka, split)
    unit = pb * lines + ka // split

    def core_at(e):
        return lax.rem(core + e, split)

    def device_at(r, e):
        target = lax.rem(unit + r, units)
        return (target // lines, lax.rem(target, lines) * split + core_at(e), ha)

    others = [(r, e) for r in range(units) for e in range(split) if (r, e) != (0, 0)]

    def row_slice(which):
        return pl.ds(pl.multiple_of(which * rows, rows), rows)

    def kv_copy(r, e):
        return pltpu.make_async_remote_copy(
            src_ref=kv_stage.at[core_at(e)],
            dst_ref=kv.at[(units - r) % units, :, row_slice(core), :],
            send_sem=kv_send.at[r, e],
            recv_sem=kv_recv.at[(units - r) % units, (split - e) % split],
            device_id=device_at(r, e), device_id_type=MESH)

    def kv_arrival(r, e):
        return pltpu.make_async_remote_copy(
            src_ref=kv_stage.at[core],
            dst_ref=kv.at[r, :, row_slice(core_at(e)), :],
            send_sem=kv_send.at[r, e], recv_sem=kv_recv.at[r, e],
            device_id=device_at(r, e), device_id_type=MESH)

    def qg_copy(which):
        return pltpu.make_async_remote_copy(
            src_ref=qg_stage.at[which, core_at(1)],
            dst_ref=qg.at[which, pl.ds(heavy, heavy), :],
            send_sem=qg_send.at[which], recv_sem=qg_recv.at[which],
            device_id=device_at(0, 1), device_id_type=MESH)

    def term_copy(r, e):
        return pltpu.make_async_remote_copy(
            src_ref=parts.at[r, :, row_slice(core_at(e)), :],
            dst_ref=terms.at[(units - r) % units, core],
            send_sem=term_send.at[r, e],
            recv_sem=term_recv.at[(units - r) % units, (split - e) % split],
            device_id=device_at(r, e), device_id_type=MESH)

    def term_arrival(r, e):
        return pltpu.make_async_remote_copy(
            src_ref=parts.at[r, :, row_slice(core), :],
            dst_ref=terms.at[r, core_at(e)],
            send_sem=term_send.at[r, e], recv_sem=term_recv.at[r, e],
            device_id=device_at(r, e), device_id_type=MESH)

    def back_copy(which, ref):
        return pltpu.make_async_remote_copy(
            src_ref=back.at[which], dst_ref=ref.at[core],
            send_sem=back_send.at[which], recv_sem=back_recv.at[which],
            device_id=device_at(0, 1), device_id_type=MESH)

    def back_arrival(which, ref):
        return pltpu.make_async_remote_copy(
            src_ref=back.at[which], dst_ref=ref.at[core_at(1)],
            send_sem=back_send.at[which], recv_sem=back_recv.at[which],
            device_id=device_at(0, 1), device_id_type=MESH)

    barrier = pltpu.get_barrier_semaphore()
    for r, e in others:
        pl.semaphore_signal(barrier, inc=1, device_id=device_at(r, e), device_id_type=MESH)

    for which, ref in ((0, k_ref), (1, v_ref)):
        wide = ref[...].astype(F32)
        for h in range(split):
            kv_stage[h, which] = wide[:, h, :].astype(HALF)
    pl.semaphore_wait(barrier, len(others))
    for r, e in others:
        kv_copy(r, e).start()
    for which in range(2):
        kv[0, which, row_slice(core), :] = kv_stage[core, which]
    for which, ref in ((0, q_ref), (1, g_ref)):
        wide = ref[...].astype(F32)
        for h in range(split):
            qg_stage[which, h] = (
                wide[:, h * group:(h + 1) * group, :].reshape(heavy, depth).astype(HALF))
        if split > 1:
            qg_copy(which).start()
        qg[which, pl.ds(0, heavy), :] = qg_stage[which, core]

    def block_rows(b):
        return pl.ds(pl.multiple_of(b * width, width), width)

    def visit(r, first, last):
        def step(b, carry):
            at = block_rows(b)
            s = lax.dot_general(kv[r, 0], qg[0, at, :], NT, preferred_element_type=F32)
            scores[b, r] = s
            top = fold_rows(s, jnp.max)
            tops[b] = top if r == 0 else jnp.maximum(tops[b], top)
            grad_probs[b, r] = lax.dot_general(
                kv[r, 1], qg[1, at, :], NT, preferred_element_type=F32)
            return carry
        lax.fori_loop(first, last, step, 0)

    for r in range(units):
        for e in range(split):
            if (r, e) != (0, 0):
                kv_arrival(r, e).wait_recv()
        for which in range(2):
            kv_t[r, which] = kv[r, which].astype(F32).T.astype(HALF)
        if r == 0:
            visit(0, 0, half_blocks)
            if split > 1:
                for which in range(2):
                    qg_copy(which).wait_recv()
                visit(0, half_blocks, blocks)
        else:
            visit(r, 0, blocks)

    def weigh(b, carry):
        top = jnp.max(tops[b], axis=0, keepdims=True) * exponent
        total = jnp.zeros((8, width), F32)
        dot = jnp.zeros((8, width), F32)
        for r in range(units):
            weights = jnp.exp2(scores[b, r] * exponent - top)
            scores[b, r] = weights
            total = total + fold_rows(weights, jnp.sum)
            dot = dot + fold_rows(weights * grad_probs[b, r], jnp.sum)
        inv = 1.0 / jnp.sum(total, axis=0, keepdims=True)
        inverse[b] = jnp.broadcast_to(inv, (8, width))
        dots[b] = jnp.broadcast_to(jnp.sum(dot, axis=0, keepdims=True) * inv, (8, width))
        return carry

    lax.fori_loop(0, blocks, weigh, 0)

    order = list(range(1, units)) + [0]
    span = rows * split
    for r in order:
        def step(b, carry):
            dk, dv = carry
            at = block_rows(b)
            probs = scores[b, r] * inverse[b, 0:1]
            prob_half = probs.astype(HALF)
            grad_scores = (probs * (grad_probs[b, r] - dots[b, 0:1])).astype(HALF)
            dv = dv + jnp.dot(prob_half, qg[1, at, :], preferred_element_type=F32)
            dk = dk + jnp.dot(grad_scores, qg[0, at, :], preferred_element_type=F32)
            o = jnp.dot(kv_t[r, 1], prob_half, preferred_element_type=F32)
            d = jnp.dot(kv_t[r, 0], grad_scores, preferred_element_type=F32)
            out_t[b] = o if r == order[0] else out_t[b] + o
            dq_t[b] = d if r == order[0] else dq_t[b] + d
            return dk, dv
        zero = jnp.zeros((span, depth), F32)
        dk, dv = lax.fori_loop(0, blocks, step, (zero, zero))
        parts[r, 0] = (dk * scaling).astype(HALF)
        parts[r, 1] = dv.astype(HALF)
        for e in range(split):
            if (r, e) != (0, 0):
                term_copy(r, e).start()
    terms[0, core] = parts[0, :, row_slice(core), :]

    for b in range(half_blocks, blocks):
        at = pl.ds((b - half_blocks) * width, width)
        back[0, at, :] = out_t[b].T.astype(HALF)
    if split > 1:
        back_copy(0, out_ref).start()
    for b in range(half_blocks, blocks):
        at = pl.ds((b - half_blocks) * width, width)
        back[1, at, :] = (dq_t[b] * scaling).T.astype(HALF)
    if split > 1:
        back_copy(1, dq_ref).start()
    for b in range(half_blocks):
        at = pl.ds(b * width, width)
        out_ref[core, at, :] = out_t[b].T.astype(HALF)
        dq_ref[core, at, :] = (dq_t[b] * scaling).T.astype(HALF)

    for r, e in others:
        term_arrival(r, e).wait_recv()
    for h in range(split):
        for which, ref in ((0, dk_ref), (1, dv_ref)):
            total = terms[0, h, which].astype(F32)
            for r in range(1, units):
                total = total + terms[r, h, which].astype(F32)
            ref[h] = total.astype(HALF)
    if split > 1:
        back_arrival(0, out_ref).wait_recv()
        back_arrival(1, dq_ref).wait_recv()
        for which, ref in ((0, out_ref), (1, dq_ref)):
            qg_copy(which).wait_send()
            back_copy(which, ref).wait_send()
    for r, e in others:
        kv_copy(r, e).wait_send()
        term_copy(r, e).wait_send()


def solution(mesh):
    pb_size, ka_size = mesh.shape["pb"], mesh.shape["ka"]

    def on_device(queries, keys, values, out_grad):
        rows, heads, depth = queries.shape
        split = keys.shape[1]
        group = heads // split
        units = pb_size * ka_size // split
        heavy = rows * group
        width = math.gcd(heavy, 512)
        blocks = split * heavy // width
        span = rows * split
        dma, vmem = pltpu.SemaphoreType.DMA, pltpu.VMEM
        in_vmem = pl.BlockSpec(memory_space=pltpu.VMEM)
        shape = jax.ShapeDtypeStruct
        out, dq, dk, dv = pl.pallas_call(
            functools.partial(kernel, (pb_size, ka_size, split, group, width)),
            out_shape=[shape((split, heavy, depth), HALF)] * 2 + [shape((split, rows, depth), HALF)] * 2,
            in_specs=[in_vmem] * 4,
            out_specs=[in_vmem] * 4,
            scratch_shapes=[
                vmem((split, 2, rows, depth), HALF),
                vmem((units, 2, span, depth), HALF),
                vmem((units, 2, depth, span), HALF),
                vmem((2, split, heavy, depth), HALF),
                vmem((2, split * heavy, depth), HALF),
                vmem((blocks, units, span, width), F32),
                vmem((blocks, units, span, width), F32),
                vmem((blocks, 8, width), F32),
                vmem((blocks, 8, width), F32),
                vmem((blocks, 8, width), F32),
                vmem((blocks, depth, width), F32),
                vmem((blocks, depth, width), F32),
                vmem((2, heavy, depth), HALF),
                vmem((units, 2, span, depth), HALF),
                vmem((units, split, 2, rows, depth), HALF),
                dma((units, split)), dma((units, split)), dma((2,)), dma((2,)),
                dma((units, split)), dma((units, split)), dma((2,)), dma((2,)),
            ],
            compiler_params=pltpu.CompilerParams(
                collective_id=0, has_side_effects=True, vmem_limit_bytes=58 * 2 ** 20),
            name="attention",
        )(keys, values, queries, out_grad)

        def by_row(x):
            wide = x.reshape(split, rows, group, depth)
            return jnp.transpose(wide, (1, 0, 2, 3)).reshape(rows, heads, depth)

        return (by_row(out), by_row(dq), jnp.transpose(dk, (1, 0, 2)), jnp.transpose(dv, (1, 0, 2)))

    spec = P(("pb", "ka"), "ha", None)
    return jax.shard_map(
        on_device, mesh=mesh, in_specs=(spec,) * 4, out_specs=(spec,) * 4, check_vma=False)
```

time: 119 us -> 34.6 us (0.29)
  blocking collectives: 73.8 us -> 0 us
  Pallas kernels: 0 us -> 29.8 us
  matrix products: 17.5 us -> 0 us
  local copies, waits for them, and re-layouts: 18.4 us -> 3.92 us
  other arithmetic: 4.05 us -> 0 us
  loops' own time: 2.93 us -> 0 us
    unnamed x1 -> x0, blocking collectives: 52.7 us -> none
    pallas_call x0 -> x1, Pallas kernels: none -> 29.8 us  [on_device(): pl.pallas_call(functools.partial(kernel, (pb_size, ka_size, split, group,...]
    all_gather x2 -> x0, blocking collectives: 21.1 us -> none  [the longest x1 11.3 us: on_device(): lax.all_gather(values, ('pb', 'ka'), axis=0, tiled=True)]
    dot_general x14 -> x0, matrix products: 17.5 us -> none  [the longest x2 7.71 us: absorb(): jnp.einsum('hgqk,khd->hgqd', weights, value_piece.astype(jnp.float32), pr...]
    while x26 -> x0, local copies, waits for them, and re-layouts: 4.89 us -> none
    unnamed x7 -> x6, local copies, waits for them, and re-layouts: 5.31 us -> 1.54 us
    another operation x2 -> x0, loops' own time: 2.93 us -> none  [the longest x1 1.46 us: on_device(): lax.scan(visit_keys, start_stats(kv_count, local_rows), jnp.arange(key_to...]
    dot_general x1 -> x0, other arithmetic: 2.52 us -> none  [on_device(): jnp.einsum('hgqd,qhgd->hgq', exact_out, grad_heads.astype(jnp.float32), p...]
where the time goes in v1:
time: 34.6 us; the launch traced here: 34.4 us
  Pallas kernels  29.8 us (86%)
  local copies, waits for them, and re-layouts  3.92 us (11%)
  between operations  0.65 us (2%)
    pallas_call x1, Pallas kernels, on_device(): pl.pallas_call(functools.partial(kernel, (pb_size, ka_size, split, group,...  29.8 us
    reshape x1, local copies, waits for them, and re-layouts, by_row(): return jnp.transpose(wide, (1, 0, 2, 3)).reshape(rows, heads, depth)  2.38 us
    unnamed x6, local copies, waits for them, and re-layouts  1.54 us

profile of v1, /device:TPU:0, one launch (start us, length us, event | category | flops | bytes accessed | tf_op | source)
XLA Modules:
  0.0 34.4 jit_solution(2188834619722258283)
XLA Ops:
  0.6 29.8 %attention.1 = (bf16[2,1024,128]{2,1,0:T(8,128)(2,1)}, bf16[2,1024,128]{2,1,0:T(8,128)(2,1)}, bf16[2,128,128]{2,1,0:T(8,128)(2,1)}, bf16[2,128,128]{2,1,0:T(8,128)(2,1)}) custom-call(bf16[128,2,128]{2,1,0:T(2,128)(2,1)} %k_ref.1, bf16[128,2,128]{2,1,0:T(2,128)(2,1)} %v_ref.1, bf16[128,16,128]{2,1,0:T(8,128)(2,1)} %q_ref.1, bf16[128,16,128]{2,1,0:T(8,128)(2,1)} %g_ref.1), custom_call_target="tpu_custom_call" | custom-call | tf_op jit(solution)/shard_map/attention/pallas_call | solution.py:243
  30.5 0.0 copy-start.1
  30.5 2.4 %copy_bitcast_fusion = (bf16[128,16,128]{2,1,0:T(8,128)(2,1)}, bf16[128,16,128]{2,1,0:T(8,128)(2,1)}) fusion(bf16[2,1024,128]{2,1,0:T(8,128)(2,1)} %get-tuple-element.8, bf16[2,1024,128]{2,1,0:T(8,128)(2,1)} %get-tuple-element.9), kind=kLoop, calls=%fused_computation | loop fusion | bytes 2097152 | tf_op jit(solution)/shard_map/reshape | solution.py:274
  32.8 0.0 copy-done.1
  32.9 0.0 copy-start
  32.9 0.7 %copy.10 = bf16[128,2,128]{2,1,0:T(2,128)(2,1)} copy(bf16[128,2,128]{2,0,1:T(8,128)(2,1)S(1)} %bitcast.17) | data formatting | bytes 131072
  33.6 0.1 copy-done
  33.7 0.7 %copy.11 = bf16[128,2,128]{2,1,0:T(2,128)(2,1)} copy(bf16[128,2,128]{2,0,1:T(8,128)(2,1)S(1)} %bitcast.16) | data formatting | bytes 131072
Async XLA Ops:
  30.5 2.4 %copy-start.1 = (bf16[2,128,128]{2,1,0:T(8,128)(2,1)S(1)}, bf16[2,128,128]{2,1,0:T(8,128)(2,1)}, u32[]{:S(2)}) copy-start(bf16[2,128,128]{2,1,0:T(8,128)(2,1)} %get-tuple-element.10) | copy-start | bytes 196612
  32.9 0.8 %copy-start = (bf16[2,128,128]{2,1,0:T(8,128)(2,1)S(1)}, bf16[2,128,128]{2,1,0:T(8,128)(2,1)}, u32[]{:S(2)}) copy-start(bf16[2,128,128]{2,1,0:T(8,128)(2,1)} %get-tuple-element.11) | copy-start | bytes 196612

commit v2 on v1

--- a/solution.py
+++ b/solution.py
@@ -18,9 +18,10 @@
     return op(x.reshape(x.shape[0] // 8, 8, x.shape[1]), axis=0)
 
 
-def kernel(dims, k_ref, v_ref, q_ref, g_ref, out_ref, dq_ref, dk_ref, dv_ref,
+def kernel(dims, k_hbm, v_hbm, q_hbm, g_hbm, out_ref, dq_ref, dk_ref, dv_ref,
+           k_ref, v_ref, q_ref, g_ref, load_sem,
            kv_stage, kv, kv_t, qg_stage, qg, scores, grad_probs, tops, inverse, dots,
-           out_t, dq_t, back, parts, terms,
+           out_t, dq_t, back, heads_out, parts, terms,
            kv_send, kv_recv, qg_send, qg_recv, term_send, term_recv, back_send, back_recv):
     pb_size, ka_size, split, group, width = dims
     rows = k_ref.shape[0]
@@ -35,14 +36,17 @@
 
     pb, ka, ha = lax.axis_index("pb"), lax.axis_index("ka"), lax.axis_index("ha")
     core = lax.rem(ka, split)
-    unit = pb * lines + ka // split
+    line = ka // split
 
     def core_at(e):
         return lax.rem(core + e, split)
 
     def device_at(r, e):
-        target = lax.rem(unit + r, units)
-        return (target // lines, lax.rem(target, lines) * split + core_at(e), ha)
+        to_pb = lax.rem(pb + r // lines, pb_size)
+        return (to_pb, lax.rem(line + r % lines, lines) * split + core_at(e), ha)
+
+    def mirror(r):
+        return (pb_size - r // lines) % pb_size * lines + (lines - r % lines) % lines
 
     others = [(r, e) for r in range(units) for e in range(split) if (r, e) != (0, 0)]
 
@@ -52,9 +56,9 @@
     def kv_copy(r, e):
         return pltpu.make_async_remote_copy(
             src_ref=kv_stage.at[core_at(e)],
-            dst_ref=kv.at[(units - r) % units, :, row_slice(core), :],
+            dst_ref=kv.at[mirror(r), :, row_slice(core), :],
             send_sem=kv_send.at[r, e],
-            recv_sem=kv_recv.at[(units - r) % units, (split - e) % split],
+            recv_sem=kv_recv.at[mirror(r), (split - e) % split],
             device_id=device_at(r, e), device_id_type=MESH)
 
     def kv_arrival(r, e):
@@ -74,9 +78,9 @@
     def term_copy(r, e):
         return pltpu.make_async_remote_copy(
             src_ref=parts.at[r, :, row_slice(core_at(e)), :],
-            dst_ref=terms.at[(units - r) % units, core],
+            dst_ref=terms.at[mirror(r), core],
             send_sem=term_send.at[r, e],
-            recv_sem=term_recv.at[(units - r) % units, (split - e) % split],
+            recv_sem=term_recv.at[mirror(r), (split - e) % split],
             device_id=device_at(r, e), device_id_type=MESH)
 
     def term_arrival(r, e):
@@ -86,23 +90,31 @@
             send_sem=term_send.at[r, e], recv_sem=term_recv.at[r, e],
             device_id=device_at(r, e), device_id_type=MESH)
 
-    def back_copy(which, ref):
-        return pltpu.make_async_remote_copy(
-            src_ref=back.at[which], dst_ref=ref.at[core],
+    def back_copy(which):
+        return pltpu.make_async_remote_copy(
+            src_ref=back.at[which], dst_ref=heads_out.at[which, core],
             send_sem=back_send.at[which], recv_sem=back_recv.at[which],
             device_id=device_at(0, 1), device_id_type=MESH)
 
-    def back_arrival(which, ref):
-        return pltpu.make_async_remote_copy(
-            src_ref=back.at[which], dst_ref=ref.at[core_at(1)],
+    def back_arrival(which):
+        return pltpu.make_async_remote_copy(
+            src_ref=back.at[which], dst_ref=heads_out.at[which, core_at(1)],
             send_sem=back_send.at[which], recv_sem=back_recv.at[which],
             device_id=device_at(0, 1), device_id_type=MESH)
 
+    loads = [
+        pltpu.make_async_copy(source, target, load_sem.at[i])
+        for i, (source, target) in enumerate(
+            ((k_hbm, k_ref), (v_hbm, v_ref), (q_hbm, q_ref), (g_hbm, g_ref)))
+    ]
+    for load in loads:
+        load.start()
     barrier = pltpu.get_barrier_semaphore()
     for r, e in others:
         pl.semaphore_signal(barrier, inc=1, device_id=device_at(r, e), device_id_type=MESH)
 
     for which, ref in ((0, k_ref), (1, v_ref)):
+        loads[which].wait()
         wide = ref[...].astype(F32)
         for h in range(split):
             kv_stage[h, which] = wide[:, h, :].astype(HALF)
@@ -112,6 +124,7 @@
     for which in range(2):
         kv[0, which, row_slice(core), :] = kv_stage[core, which]
     for which, ref in ((0, q_ref), (1, g_ref)):
+        loads[2 + which].wait()
         wide = ref[...].astype(F32)
         for h in range(split):
             qg_stage[which, h] = (
@@ -133,7 +146,7 @@
             grad_probs[b, r] = lax.dot_general(
                 kv[r, 1], qg[1, at, :], NT, preferred_element_type=F32)
             return carry
-        lax.fori_loop(first, last, step, 0)
+        lax.fori_loop(first, last, step, 0, unroll=True)
 
     for r in range(units):
         for e in range(split):
@@ -164,7 +177,7 @@
         dots[b] = jnp.broadcast_to(jnp.sum(dot, axis=0, keepdims=True) * inv, (8, width))
         return carry
 
-    lax.fori_loop(0, blocks, weigh, 0)
+    lax.fori_loop(0, blocks, weigh, 0, unroll=True)
 
     order = list(range(1, units)) + [0]
     span = rows * split
@@ -183,7 +196,7 @@
             dq_t[b] = d if r == order[0] else dq_t[b] + d
             return dk, dv
         zero = jnp.zeros((span, depth), F32)
-        dk, dv = lax.fori_loop(0, blocks, step, (zero, zero))
+        dk, dv = lax.fori_loop(0, blocks, step, (zero, zero), unroll=True)
         parts[r, 0] = (dk * scaling).astype(HALF)
         parts[r, 1] = dv.astype(HALF)
         for e in range(split):
@@ -195,34 +208,48 @@
         at = pl.ds((b - half_blocks) * width, width)
         back[0, at, :] = out_t[b].T.astype(HALF)
     if split > 1:
-        back_copy(0, out_ref).start()
+        back_copy(0).start()
     for b in range(half_blocks, blocks):
         at = pl.ds((b - half_blocks) * width, width)
         back[1, at, :] = (dq_t[b] * scaling).T.astype(HALF)
     if split > 1:
-        back_copy(1, dq_ref).start()
+        back_copy(1).start()
     for b in range(half_blocks):
         at = pl.ds(b * width, width)
-        out_ref[core, at, :] = out_t[b].T.astype(HALF)
-        dq_ref[core, at, :] = (dq_t[b] * scaling).T.astype(HALF)
+        heads_out[0, core, at, :] = out_t[b].T.astype(HALF)
+        heads_out[1, core, at, :] = (dq_t[b] * scaling).T.astype(HALF)
 
     for r, e in others:
         term_arrival(r, e).wait_recv()
-    for h in range(split):
-        for which, ref in ((0, dk_ref), (1, dv_ref)):
+    for which, ref in ((0, dk_ref), (1, dv_ref)):
+        sums = []
+        for h in range(split):
             total = terms[0, h, which].astype(F32)
             for r in range(1, units):
                 total = total + terms[r, h, which].astype(F32)
-            ref[h] = total.astype(HALF)
-    if split > 1:
-        back_arrival(0, out_ref).wait_recv()
-        back_arrival(1, dq_ref).wait_recv()
-        for which, ref in ((0, out_ref), (1, dq_ref)):
+            sums.append(total.reshape(rows, 1, depth))
+        ref[...] = jnp.concatenate(sums, axis=1).astype(HALF)
+    for which, ref in ((0, out_ref), (1, dq_ref)):
+        if split > 1:
+            back_arrival(which).wait_recv()
+        ref[...] = jnp.concatenate(
+            [heads_out[which, h].astype(F32).reshape(rows, group, depth) for h in range(split)],
+            axis=1).astype(HALF)
+        if split > 1:
             qg_copy(which).wait_send()
-            back_copy(which, ref).wait_send()
+            back_copy(which).wait_send()
     for r, e in others:
         kv_copy(r, e).wait_send()
         term_copy(r, e).wait_send()
+
+
+def hand_over(*refs):
+    count = (len(refs) - 1) // 2
+    copies = [pltpu.make_async_copy(refs[i], refs[count + i], refs[-1].at[i]) for i in range(count)]
+    for copy in copies:
+        copy.start()
+    for copy in copies:
+        copy.wait()
 
 
 def solution(mesh):
@@ -239,13 +266,16 @@
         span = rows * split
         dma, vmem = pltpu.SemaphoreType.DMA, pltpu.VMEM
         in_vmem = pl.BlockSpec(memory_space=pltpu.VMEM)
-        shape = jax.ShapeDtypeStruct
-        out, dq, dk, dv = pl.pallas_call(
+        results = [jax.ShapeDtypeStruct(x.shape, HALF) for x in (queries, queries, keys, values)]
+        stored = 8 * blocks * units * span * width
+        made = pl.pallas_call(
             functools.partial(kernel, (pb_size, ka_size, split, group, width)),
-            out_shape=[shape((split, heavy, depth), HALF)] * 2 + [shape((split, rows, depth), HALF)] * 2,
-            in_specs=[in_vmem] * 4,
+            out_shape=results,
+            in_specs=[pl.BlockSpec(memory_space=pltpu.HBM)] * 4,
             out_specs=[in_vmem] * 4,
             scratch_shapes=[
+                *[vmem(x.shape, HALF) for x in (keys, values, queries, out_grad)],
+                dma((4,)),
                 vmem((split, 2, rows, depth), HALF),
                 vmem((units, 2, span, depth), HALF),
                 vmem((units, 2, depth, span), HALF),
@@ -259,21 +289,26 @@
                 vmem((blocks, depth, width), F32),
                 vmem((blocks, depth, width), F32),
                 vmem((2, heavy, depth), HALF),
+                vmem((2, split, heavy, depth), HALF),
                 vmem((units, 2, span, depth), HALF),
                 vmem((units, split, 2, rows, depth), HALF),
                 dma((units, split)), dma((units, split)), dma((2,)), dma((2,)),
                 dma((units, split)), dma((units, split)), dma((2,)), dma((2,)),
             ],
             compiler_params=pltpu.CompilerParams(
-                collective_id=0, has_side_effects=True, vmem_limit_bytes=58 * 2 ** 20),
+                collective_id=0, has_side_effects=True, vmem_limit_bytes=stored + 16 * 2 ** 20),
             name="attention",
         )(keys, values, queries, out_grad)
 
-        def by_row(x):
-            wide = x.reshape(split, rows, group, depth)
-            return jnp.transpose(wide, (1, 0, 2, 3)).reshape(rows, heads, depth)
-
-        return (by_row(out), by_row(dq), jnp.transpose(dk, (1, 0, 2)), jnp.transpose(dv, (1, 0, 2)))
+        anywhere = pl.BlockSpec(memory_space=pl.ANY)
+        return tuple(pl.pallas_call(
+            hand_over,
+            out_shape=results,
+            in_specs=[anywhere] * 4,
+            out_specs=[anywhere] * 4,
+            scratch_shapes=[dma((4,))],
+            name="hand_over",
+        )(*made))
 
     spec = P(("pb", "ka"), "ha", None)
     return jax.shard_map(

time: 34.6 us -> 70 us (2.02)
  Pallas kernels: 29.8 us -> 62.4 us
  local copies, waits for them, and re-layouts: 3.92 us -> 6.6 us
    pallas_call x0 -> x1, Pallas kernels: none -> 36.9 us  [on_device(): pl.pallas_call(hand_over, out_shape=results, in_specs=[anywhere] * 4, out...]
    unnamed x6 -> x16, local copies, waits for them, and re-layouts: 1.54 us -> 6.6 us
    pallas_call x1, Pallas kernels: 29.8 us -> 25.5 us  [on_device(): pl.pallas_call(functools.partial(kernel, (pb_size, ka_size, split, group,...]
    reshape x1 -> x0, local copies, waits for them, and re-layouts: 2.38 us -> none  [by_row(): return jnp.transpose(wide, (1, 0, 2, 3)).reshape(rows, heads, depth)]
where the time goes in v2:
time: 70 us; the launch traced here: 69.6 us
  Pallas kernels  62.4 us (89%)
  local copies, waits for them, and re-layouts  6.6 us (9%)
    pallas_call x1, Pallas kernels, on_device(): pl.pallas_call(hand_over, out_shape=results, in_specs=[anywhere] * 4, out...  36.9 us
    pallas_call x1, Pallas kernels, on_device(): pl.pallas_call(functools.partial(kernel, (pb_size, ka_size, split, group,...  25.5 us
    unnamed x16, local copies, waits for them, and re-layouts  6.6 us

profile of v2, /device:TPU:0, one launch (start us, length us, event | category | flops | bytes accessed | tf_op | source)
XLA Modules:
  0.0 69.6 jit_solution(4824942480527768342)
XLA Ops:
  0.6 0.0 copy-start
  0.6 1.0 %copy-done = bf16[128,16,128]{2,1,0:T(8,128)(2,1)S(1)} copy-done((bf16[128,16,128]{2,1,0:T(8,128)(2,1)S(1)}, bf16[128,16,128]{2,1,0:T(8,128)(2,1)}, u32[]{:S(2)}) %copy-start) | copy-done | bytes 524312
  1.7 0.0 copy-start.1
  1.7 1.0 %copy-done.1 = bf16[128,16,128]{2,1,0:T(8,128)(2,1)S(1)} copy-done((bf16[128,16,128]{2,1,0:T(8,128)(2,1)S(1)}, bf16[128,16,128]{2,1,0:T(8,128)(2,1)}, u32[]{:S(2)}) %copy-start.1) | copy-done | bytes 524312
  2.7 0.0 copy-start.4
  2.7 0.8 %copy-done.4 = bf16[128,2,128]{2,1,0:T(2,128)(2,1)S(1)} copy-done((bf16[128,2,128]{2,1,0:T(2,128)(2,1)S(1)}, bf16[128,2,128]{2,1,0:T(2,128)(2,1)}, u32[]{:S(2)}) %copy-start.4) | copy-done | bytes 65560
  3.6 0.0 copy-start.5
  3.6 0.8 %copy-done.5 = bf16[128,2,128]{2,1,0:T(2,128)(2,1)S(1)} copy-done((bf16[128,2,128]{2,1,0:T(2,128)(2,1)S(1)}, bf16[128,2,128]{2,1,0:T(2,128)(2,1)}, u32[]{:S(2)}) %copy-start.5) | copy-done | bytes 65560
  4.4 25.5 %attention.1 = (bf16[128,16,128]{2,1,0:T(8,128)(2,1)S(1)}, bf16[128,16,128]{2,1,0:T(8,128)(2,1)S(1)}, bf16[128,2,128]{2,1,0:T(2,128)(2,1)S(1)}, bf16[128,2,128]{2,1,0:T(2,128)(2,1)S(1)}) custom-call(bf16[128,2,128]{2,1,0:T(2,128)(2,1)S(1)} %copy-done.4, bf16[128,2,128]{2,1,0:T(2,128)(2,1)S(1)} %copy-done.5, bf16[128,16,128]{2,1,0:T(8,128)(2,1)S(1)} %copy-done, ...), custom_call_target="tpu_custom_call" | custom-call | tf_op jit(solution)/shard_map/attention/pallas_call | solution.py:271
  29.9 0.0 copy-start.2
  29.9 0.8 %copy-done.2 = bf16[128,16,128]{2,1,0:T(8,128)(2,1)} copy-done((bf16[128,16,128]{2,1,0:T(8,128)(2,1)}, bf16[128,16,128]{2,1,0:T(8,128)(2,1)S(1)}, u32[]{:S(2)}) %copy-start.2) | copy-done | bytes 524312
  30.7 0.0 copy-start.3
  30.7 0.8 %copy-done.3 = bf16[128,16,128]{2,1,0:T(8,128)(2,1)} copy-done((bf16[128,16,128]{2,1,0:T(8,128)(2,1)}, bf16[128,16,128]{2,1,0:T(8,128)(2,1)S(1)}, u32[]{:S(2)}) %copy-start.3) | copy-done | bytes 524312
  31.5 0.0 copy-start.6
  31.5 0.6 copy-done.6
  32.1 0.0 copy-start.7
  32.2 0.6 copy-done.7
  32.8 36.9 %hand_over.1 = (bf16[128,16,128]{2,1,0:T(8,128)(2,1)}, bf16[128,16,128]{2,1,0:T(8,128)(2,1)}, bf16[128,2,128]{2,1,0:T(2,128)(2,1)}, bf16[128,2,128]{2,1,0:T(2,128)(2,1)}) custom-call(bf16[128,16,128]{2,1,0:T(8,128)(2,1)} %copy-done.2, bf16[128,16,128]{2,1,0:T(8,128)(2,1)} %copy-done.3, bf16[128,2,128]{2,1,0:T(2,128)(2,1)} %copy-done.6, ...), custom_call_target="tpu_custom_call" | custom-call | tf_op jit(solution)/shard_map/hand_over/pallas_call | solution.py:304
Async XLA Ops:
  0.6 1.0 %copy-start = (bf16[128,16,128]{2,1,0:T(8,128)(2,1)S(1)}, bf16[128,16,128]{2,1,0:T(8,128)(2,1)}, u32[]{:S(2)}) copy-start(bf16[128,16,128]{2,1,0:T(8,128)(2,1)} %q_hbm.1) | copy-start | bytes 1572868
  1.7 1.0 %copy-start.1 = (bf16[128,16,128]{2,1,0:T(8,128)(2,1)S(1)}, bf16[128,16,128]{2,1,0:T(8,128)(2,1)}, u32[]{:S(2)}) copy-start(bf16[128,16,128]{2,1,0:T(8,128)(2,1)} %g_hbm.1) | copy-start | bytes 1572868
  2.7 0.8 %copy-start.4 = (bf16[128,2,128]{2,1,0:T(2,128)(2,1)S(1)}, bf16[128,2,128]{2,1,0:T(2,128)(2,1)}, u32[]{:S(2)}) copy-start(bf16[128,2,128]{2,1,0:T(2,128)(2,1)} %k_hbm.1) | copy-start | bytes 196612
  3.6 0.8 %copy-start.5 = (bf16[128,2,128]{2,1,0:T(2,128)(2,1)S(1)}, bf16[128,2,128]{2,1,0:T(2,128)(2,1)}, u32[]{:S(2)}) copy-start(bf16[128,2,128]{2,1,0:T(2,128)(2,1)} %v_hbm.1) | copy-start | bytes 196612
  29.9 0.8 %copy-start.2 = (bf16[128,16,128]{2,1,0:T(8,128)(2,1)}, bf16[128,16,128]{2,1,0:T(8,128)(2,1)S(1)}, u32[]{:S(2)}) copy-start(bf16[128,16,128]{2,1,0:T(8,128)(2,1)S(1)} %get-tuple-element.8.refs_0_) | copy-start | bytes 1572868
  30.7 0.8 %copy-start.3 = (bf16[128,16,128]{2,1,0:T(8,128)(2,1)}, bf16[128,16,128]{2,1,0:T(8,128)(2,1)S(1)}, u32[]{:S(2)}) copy-start(bf16[128,16,128]{2,1,0:T(8,128)(2,1)S(1)} %get-tuple-element.9.refs_1_) | copy-start | bytes 1572868
  31.5 0.6 copy-start.6
  32.1 0.6 copy-start.7

commit v3 on v2

--- a/solution.py
+++ b/solution.py
@@ -18,8 +18,8 @@
     return op(x.reshape(x.shape[0] // 8, 8, x.shape[1]), axis=0)
 
 
-def kernel(dims, k_hbm, v_hbm, q_hbm, g_hbm, out_ref, dq_ref, dk_ref, dv_ref,
-           k_ref, v_ref, q_ref, g_ref, load_sem,
+def kernel(dims, k_hbm, v_hbm, q_hbm, g_hbm, out_hbm, dq_hbm, dk_hbm, dv_hbm,
+           k_ref, v_ref, q_ref, g_ref, out_ref, dq_ref, dk_ref, dv_ref, load_sem, store_sem,
            kv_stage, kv, kv_t, qg_stage, qg, scores, grad_probs, tops, inverse, dots,
            out_t, dq_t, back, heads_out, parts, terms,
            kv_send, kv_recv, qg_send, qg_recv, term_send, term_recv, back_send, back_recv):
@@ -48,24 +48,31 @@
     def mirror(r):
         return (pb_size - r // lines) % pb_size * lines + (lines - r % lines) % lines
 
+    def far(r):
+        return min(r // lines, pb_size - r // lines) + min(r % lines, lines - r % lines)
+
     others = [(r, e) for r in range(units) for e in range(split) if (r, e) != (0, 0)]
+
+    near = sorted(others, key=lambda at: far(at[0]))
+    siblings = [at for at in near if at[0] == 0]
+    farthest = siblings + [at for at in reversed(near) if at[0] != 0]
 
     def row_slice(which):
         return pl.ds(pl.multiple_of(which * rows, rows), rows)
 
-    def kv_copy(r, e):
-        return pltpu.make_async_remote_copy(
-            src_ref=kv_stage.at[core_at(e)],
-            dst_ref=kv.at[mirror(r), :, row_slice(core), :],
-            send_sem=kv_send.at[r, e],
-            recv_sem=kv_recv.at[mirror(r), (split - e) % split],
+    def kv_copy(which, r, e):
+        return pltpu.make_async_remote_copy(
+            src_ref=kv_stage.at[which, core_at(e)],
+            dst_ref=kv.at[mirror(r), which, row_slice(core), :],
+            send_sem=kv_send.at[which, r, e],
+            recv_sem=kv_recv.at[which, mirror(r), (split - e) % split],
             device_id=device_at(r, e), device_id_type=MESH)
 
-    def kv_arrival(r, e):
-        return pltpu.make_async_remote_copy(
-            src_ref=kv_stage.at[core],
-            dst_ref=kv.at[r, :, row_slice(core_at(e)), :],
-            send_sem=kv_send.at[r, e], recv_sem=kv_recv.at[r, e],
+    def kv_arrival(which, r, e):
+        return pltpu.make_async_remote_copy(
+            src_ref=kv_stage.at[which, core],
+            dst_ref=kv.at[r, which, row_slice(core_at(e)), :],
+            send_sem=kv_send.at[which, r, e], recv_sem=kv_recv.at[which, r, e],
             device_id=device_at(r, e), device_id_type=MESH)
 
     def qg_copy(which):
@@ -117,12 +124,12 @@
         loads[which].wait()
         wide = ref[...].astype(F32)
         for h in range(split):
-            kv_stage[h, which] = wide[:, h, :].astype(HALF)
-    pl.semaphore_wait(barrier, len(others))
-    for r, e in others:
-        kv_copy(r, e).start()
-    for which in range(2):
-        kv[0, which, row_slice(core), :] = kv_stage[core, which]
+            kv_stage[which, h] = wide[:, h, :].astype(HALF)
+        if which == 0:
+            pl.semaphore_wait(barrier, len(others))
+        for r, e in farthest:
+            kv_copy(which, r, e).start()
+        kv[0, which, row_slice(core), :] = kv_stage[which, core]
     for which, ref in ((0, q_ref), (1, g_ref)):
         loads[2 + which].wait()
         wide = ref[...].astype(F32)
@@ -134,56 +141,67 @@
         qg[which, pl.ds(0, heavy), :] = qg_stage[which, core]
 
     def block_rows(b):
-        return pl.ds(pl.multiple_of(b * width, width), width)
-
-    def visit(r, first, last):
-        def step(b, carry):
-            at = block_rows(b)
-            s = lax.dot_general(kv[r, 0], qg[0, at, :], NT, preferred_element_type=F32)
+        return pl.ds(b * width, width)
+
+    def arrive(which, r):
+        for e in range(split):
+            if (r, e) != (0, 0):
+                kv_arrival(which, r, e).wait_recv()
+
+    def score(r, first, last):
+        for b in range(first, last):
+            s = lax.dot_general(
+                kv[r, 0], qg[0, block_rows(b), :], NT, preferred_element_type=F32)
             scores[b, r] = s
             top = fold_rows(s, jnp.max)
             tops[b] = top if r == 0 else jnp.maximum(tops[b], top)
-            grad_probs[b, r] = lax.dot_general(
-                kv[r, 1], qg[1, at, :], NT, preferred_element_type=F32)
-            return carry
-        lax.fori_loop(first, last, step, 0, unroll=True)
-
-    for r in range(units):
-        for e in range(split):
-            if (r, e) != (0, 0):
-                kv_arrival(r, e).wait_recv()
-        for which in range(2):
-            kv_t[r, which] = kv[r, which].astype(F32).T.astype(HALF)
-        if r == 0:
-            visit(0, 0, half_blocks)
-            if split > 1:
-                for which in range(2):
-                    qg_copy(which).wait_recv()
-                visit(0, half_blocks, blocks)
-        else:
-            visit(r, 0, blocks)
-
-    def weigh(b, carry):
+
+    def weigh(b):
         top = jnp.max(tops[b], axis=0, keepdims=True) * exponent
         total = jnp.zeros((8, width), F32)
-        dot = jnp.zeros((8, width), F32)
         for r in range(units):
             weights = jnp.exp2(scores[b, r] * exponent - top)
             scores[b, r] = weights
             total = total + fold_rows(weights, jnp.sum)
-            dot = dot + fold_rows(weights * grad_probs[b, r], jnp.sum)
         inv = 1.0 / jnp.sum(total, axis=0, keepdims=True)
         inverse[b] = jnp.broadcast_to(inv, (8, width))
-        dots[b] = jnp.broadcast_to(jnp.sum(dot, axis=0, keepdims=True) * inv, (8, width))
-        return carry
-
-    lax.fori_loop(0, blocks, weigh, 0, unroll=True)
-
-    order = list(range(1, units)) + [0]
+
+    def grade(r, b):
+        grad = lax.dot_general(
+            kv[r, 1], qg[1, block_rows(b), :], NT, preferred_element_type=F32)
+        grad_probs[b, r] = grad
+        dot = fold_rows(scores[b, r] * grad, jnp.sum)
+        dots[b] = dot if r == 0 else dots[b] + dot
+
+    def turn(which, r):
+        kv_t[r, which] = kv[r, which].T
+
+    for r in range(units):
+        arrive(0, r)
+        score(r, 0, half_blocks if r == 0 else blocks)
+        turn(0, r)
+        if r == 0 and split > 1:
+            qg_copy(0).wait_recv()
+            score(0, half_blocks, blocks)
+    for r in range(units):
+        arrive(1, r)
+        if r == 0 and split > 1:
+            qg_copy(1).wait_recv()
+        for b in range(blocks):
+            if r == 0:
+                weigh(b)
+            grade(r, b)
+        turn(1, r)
+    for b in range(blocks):
+        dots[b] = jnp.broadcast_to(
+            jnp.sum(dots[b], axis=0, keepdims=True) * inverse[b, 0:1], (8, width))
+
+    order = sorted(range(units), key=far, reverse=True)
     span = rows * split
     for r in order:
-        def step(b, carry):
-            dk, dv = carry
+        dk = jnp.zeros((span, depth), F32)
+        dv = jnp.zeros((span, depth), F32)
+        for b in range(blocks):
             at = block_rows(b)
             probs = scores[b, r] * inverse[b, 0:1]
             prob_half = probs.astype(HALF)
@@ -194,9 +212,6 @@
             d = jnp.dot(kv_t[r, 0], grad_scores, preferred_element_type=F32)
             out_t[b] = o if r == order[0] else out_t[b] + o
             dq_t[b] = d if r == order[0] else dq_t[b] + d
-            return dk, dv
-        zero = jnp.zeros((span, depth), F32)
-        dk, dv = lax.fori_loop(0, blocks, step, (zero, zero), unroll=True)
         parts[r, 0] = (dk * scaling).astype(HALF)
         parts[r, 1] = dv.astype(HALF)
         for e in range(split):
@@ -206,19 +221,31 @@
 
     for b in range(half_blocks, blocks):
         at = pl.ds((b - half_blocks) * width, width)
-        back[0, at, :] = out_t[b].T.astype(HALF)
+        back[0, at, :] = out_t[b].astype(HALF).T
     if split > 1:
         back_copy(0).start()
     for b in range(half_blocks, blocks):
         at = pl.ds((b - half_blocks) * width, width)
-        back[1, at, :] = (dq_t[b] * scaling).T.astype(HALF)
+        back[1, at, :] = (dq_t[b] * scaling).astype(HALF).T
     if split > 1:
         back_copy(1).start()
     for b in range(half_blocks):
         at = pl.ds(b * width, width)
-        heads_out[0, core, at, :] = out_t[b].T.astype(HALF)
-        heads_out[1, core, at, :] = (dq_t[b] * scaling).T.astype(HALF)
-
+        heads_out[0, core, at, :] = out_t[b].astype(HALF).T
+        heads_out[1, core, at, :] = (dq_t[b] * scaling).astype(HALF).T
+
+    stores = [
+        pltpu.make_async_copy(source, target, store_sem.at[i])
+        for i, (source, target) in enumerate(
+            ((out_ref, out_hbm), (dq_ref, dq_hbm), (dk_ref, dk_hbm), (dv_ref, dv_hbm)))
+    ]
+    for which, ref in ((0, out_ref), (1, dq_ref)):
+        if split > 1:
+            back_arrival(which).wait_recv()
+        ref[...] = jnp.concatenate(
+            [heads_out[which, h].astype(F32).reshape(rows, group, depth) for h in range(split)],
+            axis=1).astype(HALF)
+        stores[which].start()
     for r, e in others:
         term_arrival(r, e).wait_recv()
     for which, ref in ((0, dk_ref), (1, dv_ref)):
@@ -229,17 +256,16 @@
                 total = total + terms[r, h, which].astype(F32)
             sums.append(total.reshape(rows, 1, depth))
         ref[...] = jnp.concatenate(sums, axis=1).astype(HALF)
-    for which, ref in ((0, out_ref), (1, dq_ref)):
-        if split > 1:
-            back_arrival(which).wait_recv()
-        ref[...] = jnp.concatenate(
-            [heads_out[which, h].astype(F32).reshape(rows, group, depth) for h in range(split)],
-            axis=1).astype(HALF)
-        if split > 1:
+        stores[2 + which].start()
+    for store in stores:
+        store.wait()
+    if split > 1:
+        for which in range(2):
             qg_copy(which).wait_send()
             back_copy(which).wait_send()
     for r, e in others:
-        kv_copy(r, e).wait_send()
+        for which in range(2):
+            kv_copy(which, r, e).wait_send()
         term_copy(r, e).wait_send()
 
 
@@ -266,17 +292,18 @@
         span = rows * split
         dma, vmem = pltpu.SemaphoreType.DMA, pltpu.VMEM
         in_vmem = pl.BlockSpec(memory_space=pltpu.VMEM)
+        in_hbm = pl.BlockSpec(memory_space=pltpu.HBM)
         results = [jax.ShapeDtypeStruct(x.shape, HALF) for x in (queries, queries, keys, values)]
-        stored = 8 * blocks * units * span * width
         made = pl.pallas_call(
             functools.partial(kernel, (pb_size, ka_size, split, group, width)),
             out_shape=results,
-            in_specs=[pl.BlockSpec(memory_space=pltpu.HBM)] * 4,
-            out_specs=[in_vmem] * 4,
+            in_specs=[in_hbm] * 4,
+            out_specs=[in_hbm] * 4,
             scratch_shapes=[
                 *[vmem(x.shape, HALF) for x in (keys, values, queries, out_grad)],
-                dma((4,)),
-                vmem((split, 2, rows, depth), HALF),
+                *[vmem(x.shape, HALF) for x in results],
+                dma((4,)), dma((4,)),
+                vmem((2, split, rows, depth), HALF),
                 vmem((units, 2, span, depth), HALF),
                 vmem((units, 2, depth, span), HALF),
                 vmem((2, split, heavy, depth), HALF),
@@ -292,21 +319,21 @@
                 vmem((2, split, heavy, depth), HALF),
                 vmem((units, 2, span, depth), HALF),
                 vmem((units, split, 2, rows, depth), HALF),
-                dma((units, split)), dma((units, split)), dma((2,)), dma((2,)),
+                dma((2, units, split)), dma((2, units, split)), dma((2,)), dma((2,)),
                 dma((units, split)), dma((units, split)), dma((2,)), dma((2,)),
             ],
             compiler_params=pltpu.CompilerParams(
-                collective_id=0, has_side_effects=True, vmem_limit_bytes=stored + 16 * 2 ** 20),
+                collective_id=0, has_side_effects=True, vmem_limit_bytes=58 * 2 ** 20),
             name="attention",
         )(keys, values, queries, out_grad)
 
-        anywhere = pl.BlockSpec(memory_space=pl.ANY)
         return tuple(pl.pallas_call(
             hand_over,
             out_shape=results,
-            in_specs=[anywhere] * 4,
-            out_specs=[anywhere] * 4,
+            in_specs=[in_vmem] * 4,
+            out_specs=[in_hbm] * 4,
             scratch_shapes=[dma((4,))],
+            compiler_params=pltpu.CompilerParams(vmem_limit_bytes=58 * 2 ** 20),
             name="hand_over",
         )(*made))
 

time: 70 us -> 26 us (0.37)
  Pallas kernels: 62.4 us -> 25.2 us
  local copies, waits for them, and re-layouts: 6.6 us -> 0 us
    pallas_call x1, Pallas kernels: 36.9 us -> 2.24 us  [on_device(): pl.pallas_call(hand_over, out_shape=results, in_specs=[in_vmem] * 4, out_...]
    unnamed x16 -> x0, local copies, waits for them, and re-layouts: 6.6 us -> none
    pallas_call x1, Pallas kernels: 25.5 us -> 23 us  [on_device(): pl.pallas_call(functools.partial(kernel, (pb_size, ka_size, split, group,...]
where the time goes in v3:
time: 26 us; the launch traced here: 25.8 us
  Pallas kernels  25.2 us (97%)
  between operations  0.64 us (2%)
    pallas_call x1, Pallas kernels, on_device(): pl.pallas_call(functools.partial(kernel, (pb_size, ka_size, split, group,...  23 us
    pallas_call x1, Pallas kernels, on_device(): pl.pallas_call(hand_over, out_shape=results, in_specs=[in_vmem] * 4, out_...  2.24 us

profile of v3, /device:TPU:0, one launch (start us, length us, event | category | flops | bytes accessed | tf_op | source)
XLA Modules:
  0.0 25.8 jit_solution(16630629889961283943)
XLA Ops:
  0.6 23.0 %attention.1 = (bf16[128,16,128]{2,1,0:T(8,128)(2,1)}, bf16[128,16,128]{2,1,0:T(8,128)(2,1)}, bf16[128,2,128]{2,1,0:T(2,128)(2,1)}, bf16[128,2,128]{2,1,0:T(2,128)(2,1)}) custom-call(bf16[128,2,128]{2,1,0:T(2,128)(2,1)} %k_hbm.1, bf16[128,2,128]{2,1,0:T(2,128)(2,1)} %v_hbm.1, bf16[128,16,128]{2,1,0:T(8,128)(2,1)} %q_hbm.1, bf16[128,16,128]{2,1,0:T(8,128)(2,1)} %g_hbm.1), custom_call_target="tpu_custom_call" | custom-call | tf_op jit(solution)/shard_map/attention/pallas_call | solution.py:297
  23.6 2.2 %hand_over.1 = (bf16[128,16,128]{2,1,0:T(8,128)(2,1)}, bf16[128,16,128]{2,1,0:T(8,128)(2,1)}, bf16[128,2,128]{2,1,0:T(2,128)(2,1)}, bf16[128,2,128]{2,1,0:T(2,128)(2,1)}) custom-call(bf16[128,16,128]{2,1,0:T(8,128)(2,1)} %get-tuple-element.8.refs_0_, bf16[128,16,128]{2,1,0:T(8,128)(2,1)} %get-tuple-element.9.refs_1_, ...), custom_call_target="tpu_custom_call" | custom-call | tf_op jit(solution)/shard_map/hand_over/pallas_call | solution.py:330

commit v4 on v3

v4 whole, which is shorter than its diff:
```python
import functools
import math

import jax
import jax.numpy as jnp
from jax import lax
from jax.experimental import pallas as pl
from jax.experimental.pallas import tpu as pltpu
from jax.sharding import PartitionSpec as P

MESH = pl.DeviceIdType.MESH
F32 = jnp.float32
HALF = jnp.bfloat16


def fold_rows(x, op):
    return op(x.reshape(x.shape[0] // 8, 8, x.shape[1]), axis=0)


def kernel(dims, k_hbm, v_hbm, q_hbm, g_hbm, heads_out, terms,
           k_ref, v_ref, q_ref, g_ref, kv_stage, kv, kv_t, qg_stage, qg, qg_t,
           scores, grad_probs, prob_half, sums, tops, dots, out_t, dq_t, back, parts,
           load_sem, own_sem, kv_send, kv_recv, qg_send, qg_recv,
           term_send, term_recv, back_send, back_recv):
    pb_size, ka_size, split, group, width = dims
    rows = k_ref.shape[0]
    depth = k_ref.shape[2]
    scaling = depth ** (-0.5)
    exponent = scaling * math.log2(math.e)
    lines = ka_size // split
    units = pb_size * lines
    heavy = rows * group
    blocks = split * heavy // width
    half_blocks = heavy // width

    pb, ka, ha = lax.axis_index("pb"), lax.axis_index("ka"), lax.axis_index("ha")
    core = lax.rem(ka, split)
    line = ka // split

    def core_at(e):
        return lax.rem(core + e, split)

    def device_at(r, e):
        to_pb = lax.rem(pb + r // lines, pb_size)
        return (to_pb, lax.rem(line + r % lines, lines) * split + core_at(e), ha)

    def mirror(r):
        return (pb_size - r // lines) % pb_size * lines + (lines - r % lines) % lines

    def far(r):
        return min(r // lines, pb_size - r // lines) + min(r % lines, lines - r % lines)

    others = [(r, e) for r in range(units) for e in range(split) if (r, e) != (0, 0)]

    near = sorted(others, key=lambda at: far(at[0]))
    siblings = [at for at in near if at[0] == 0]
    farthest = siblings + [at for at in reversed(near) if at[0] != 0]

    def row_slice(which):
        return pl.ds(pl.multiple_of(which * rows, rows), rows)

    def kv_copy(which, r, e):
        return pltpu.make_async_remote_copy(
            src_ref=kv_stage.at[which, core_at(e)],
            dst_ref=kv.at[mirror(r), which, row_slice(core), :],
            send_sem=kv_send.at[which, r, e],
            recv_sem=kv_recv.at[which, mirror(r), (split - e) % split],
            device_id=device_at(r, e), device_id_type=MESH)

    def kv_arrival(which, r, e):
        return pltpu.make_async_remote_copy(
            src_ref=kv_stage.at[which, core],
            dst_ref=kv.at[r, which, row_slice(core_at(e)), :],
            send_sem=kv_send.at[which, r, e], recv_sem=kv_recv.at[which, r, e],
            device_id=device_at(r, e), device_id_type=MESH)

    def qg_copy(which):
        return pltpu.make_async_remote_copy(
            src_ref=qg_stage.at[which, core_at(1)],
            dst_ref=qg.at[which, pl.ds(heavy, heavy), :],
            send_sem=qg_send.at[which], recv_sem=qg_recv.at[which],
            device_id=device_at(0, 1), device_id_type=MESH)

    def term_copy(which, r, e):
        return pltpu.make_async_remote_copy(
            src_ref=parts.at[which, r, row_slice(core_at(e)), :],
            dst_ref=terms.at[mirror(r), core, which],
            send_sem=term_send.at[which, r, e],
            recv_sem=term_recv.at[which, mirror(r), (split - e) % split],
            device_id=device_at(r, e), device_id_type=MESH)

    def term_arrival(which, r, e):
        return pltpu.make_async_remote_copy(
            src_ref=parts.at[which, r, row_slice(core), :],
            dst_ref=terms.at[r, core_at(e), which],
            send_sem=term_send.at[which, r, e], recv_sem=term_recv.at[which, r, e],
            device_id=device_at(r, e), device_id_type=MESH)

    def own_term(which):
        return pltpu.make_async_copy(
            parts.at[which, 0, row_slice(core), :], terms.at[0, core, which], own_sem.at[which])

    def own_heads(which):
        return pltpu.make_async_copy(
            back.at[which, 0], heads_out.at[which, core], own_sem.at[2 + which])

    def back_copy(which):
        return pltpu.make_async_remote_copy(
            src_ref=back.at[which, 1], dst_ref=heads_out.at[which, core],
            send_sem=back_send.at[which], recv_sem=back_recv.at[which],
            device_id=device_at(0, 1), device_id_type=MESH)

    def back_arrival(which):
        return pltpu.make_async_remote_copy(
            src_ref=back.at[which, 1], dst_ref=heads_out.at[which, core_at(1)],
            send_sem=back_send.at[which], recv_sem=back_recv.at[which],
            device_id=device_at(0, 1), device_id_type=MESH)

    loads = [
        pltpu.make_async_copy(source, target, load_sem.at[i])
        for i, (source, target) in enumerate(
            ((k_hbm, k_ref), (v_hbm, v_ref), (q_hbm, q_ref), (g_hbm, g_ref)))
    ]
    for load in loads:
        load.start()
    barrier = pltpu.get_barrier_semaphore()
    for r, e in others:
        pl.semaphore_signal(barrier, inc=1, device_id=device_at(r, e), device_id_type=MESH)

    for which, ref in ((0, k_ref), (1, v_ref)):
        loads[which].wait()
        wide = ref[...].astype(F32)
        for h in range(split):
            kv_stage[which, h] = wide[:, h, :].astype(HALF)
        if which == 0:
            pl.semaphore_wait(barrier, len(others))
        for r, e in farthest:
            kv_copy(which, r, e).start()
        kv[0, which, row_slice(core), :] = kv_stage[which, core]
    for which, ref in ((0, q_ref), (1, g_ref)):
        loads[2 + which].wait()
        wide = ref[...].astype(F32)
        for h in range(split):
            qg_stage[which, h] = (
                wide[:, h * group:(h + 1) * group, :].reshape(heavy, depth).astype(HALF))
        if split > 1:
            qg_copy(which).start()
        qg[which, pl.ds(0, heavy), :] = qg_stage[which, core]

    def block_rows(b):
        return pl.ds(b * width, width)

    def arrive(which, r):
        for e in range(split):
            if (r, e) != (0, 0):
                kv_arrival(which, r, e).wait_recv()

    def turn_block(which, b):
        qg_t[which, b] = qg[which, block_rows(b), :].T

    def score(r, first, last):
        for b in range(first, last):
            s = jnp.dot(kv[r, 0], qg_t[0, b], preferred_element_type=F32)
            scores[b, r] = s
            top = fold_rows(s, jnp.max)
            tops[b] = top if r == 0 else jnp.maximum(tops[b], top)

    def weigh(b):
        top = jnp.max(tops[b], axis=0, keepdims=True) * exponent
        total = jnp.zeros((8, width), F32)
        for r in range(units):
            weights = jnp.exp2(scores[b, r] * exponent - top)
            scores[b, r] = weights
            total = total + fold_rows(weights, jnp.sum)
        return 1.0 / jnp.sum(total, axis=0, keepdims=True)

    def value_terms(b, inverse):
        for r in range(units):
            probs = scores[b, r] * inverse
            half = probs.astype(HALF)
            scores[b, r] = probs
            prob_half[b, r] = half
            dv = jnp.dot(half, qg[1, block_rows(b), :], preferred_element_type=F32)
            sums[r] = dv if b == 0 else sums[r] + dv

    def grade(r, b):
        grad = jnp.dot(kv[r, 1], qg_t[1, b], preferred_element_type=F32)
        grad_probs[b, r] = grad
        dot = fold_rows(scores[b, r] * grad, jnp.sum)
        dots[b] = dot if r == 0 else dots[b] + dot
        out = jnp.dot(kv_t[r, 1], prob_half[b, r], preferred_element_type=F32)
        out_t[b] = out if r == 0 else out_t[b] + out

    def turn(which, r):
        kv_t[r, which] = kv[r, which].T

    def send_terms(which, r):
        for e in range(split):
            if (r, e) != (0, 0):
                term_copy(which, r, e).start()
        if r == 0:
            own_term(which).start()

    def send_heads(which, turned, scale):
        for half in reversed(range(split)):
            for b in range(half_blocks):
                back[which, half, block_rows(b), :] = (
                    (turned[half * half_blocks + b] * scale).astype(HALF).T)
            if half:
                back_copy(which).start()
            else:
                own_heads(which).start()

    for b in range(half_blocks):
        turn_block(0, b)
    arrive(0, 0)
    score(0, 0, half_blocks)
    for b in range(half_blocks):
        turn_block(1, b)
    turn(0, 0)
    if split > 1:
        qg_copy(0).wait_recv()
        for b in range(half_blocks, blocks):
            turn_block(0, b)
        score(0, half_blocks, blocks)
        qg_copy(1).wait_recv()
        for b in range(half_blocks, blocks):
            turn_block(1, b)
    for r in range(1, units):
        arrive(0, r)
        score(r, 0, blocks)
        turn(0, r)
    arrive(1, 0)
    turn(1, 0)
    for b in range(blocks):
        value_terms(b, weigh(b))
        grade(0, b)
    order = sorted(range(units), key=far, reverse=True)
    for r in order:
        parts[1, r] = sums[r].astype(HALF)
        send_terms(1, r)
    for r in range(1, units):
        arrive(1, r)
        turn(1, r)
        for b in range(blocks):
            grade(r, b)
    for b in range(blocks):
        dots[b] = jnp.broadcast_to(jnp.sum(dots[b], axis=0, keepdims=True), (8, width))
    for r in order:
        dk = jnp.zeros((rows * split, depth), F32)
        for b in range(blocks):
            grad_scores = (scores[b, r] * (grad_probs[b, r] - dots[b, 0:1])).astype(HALF)
            dk = dk + jnp.dot(grad_scores, qg[0, block_rows(b), :], preferred_element_type=F32)
            d = jnp.dot(kv_t[r, 0], grad_scores, preferred_element_type=F32)
            dq_t[b] = d if r == order[0] else dq_t[b] + d
        parts[0, r] = (dk * scaling).astype(HALF)
        send_terms(0, r)
        if r == order[0]:
            send_heads(0, out_t, 1.0)
    send_heads(1, dq_t, scaling)

    for which in range(2):
        own_term(which).wait()
        own_heads(which).wait()
        if split > 1:
            back_arrival(which).wait_recv()
            qg_copy(which).wait_send()
            back_copy(which).wait_send()
    for which in range(2):
        for r, e in others:
            kv_copy(which, r, e).wait_send()
            term_copy(which, r, e).wait_send()
    for which in (1, 0):
        for r, e in others:
            term_arrival(which, r, e).wait_recv()


def gather_up(heads_hbm, terms_hbm, out_hbm, dq_hbm, dk_hbm, dv_hbm,
              heads, terms, out_ref, dq_ref, dk_ref, dv_ref, load_sem, store_sem):
    split, heavy, depth = heads.shape[1:]
    units = terms.shape[0]
    rows = terms.shape[3]
    loads = [
        pltpu.make_async_copy(source, target, load_sem.at[i])
        for i, (source, target) in enumerate((
            (heads_hbm.at[0], heads.at[0]), (heads_hbm.at[1], heads.at[1]), (terms_hbm, terms)))
    ]
    stores = [
        pltpu.make_async_copy(source, target, store_sem.at[i])
        for i, (source, target) in enumerate(
            ((out_ref, out_hbm), (dq_ref, dq_hbm), (dk_ref, dk_hbm), (dv_ref, dv_hbm)))
    ]
    for load in loads:
        load.start()
    for which, ref in ((0, out_ref), (1, dq_ref)):
        loads[which].wait()
        ref[...] = jnp.concatenate(
            [heads[which, h].astype(F32).reshape(rows, heavy // rows, depth) for h in range(split)],
            axis=1).astype(HALF)
        stores[which].start()
    loads[2].wait()
    for which, ref in ((0, dk_ref), (1, dv_ref)):
        sums = []
        for h in range(split):
            total = terms[0, h, which].astype(F32)
            for r in range(1, units):
                total = total + terms[r, h, which].astype(F32)
            sums.append(total.reshape(rows, 1, depth))
        ref[...] = jnp.concatenate(sums, axis=1).astype(HALF)
        stores[2 + which].start()
    for store in stores:
        store.wait()


def solution(mesh):
    pb_size, ka_size = mesh.shape["pb"], mesh.shape["ka"]

    def on_device(queries, keys, values, out_grad):
        rows, heads, depth = queries.shape
        split = keys.shape[1]
        group = heads // split
        units = pb_size * ka_size // split
        heavy = rows * group
        width = math.gcd(heavy, 512)
        blocks = split * heavy // width
        span = rows * split
        dma, vmem = pltpu.SemaphoreType.DMA, pltpu.VMEM
        in_hbm = pl.BlockSpec(memory_space=pltpu.HBM)
        shape = jax.ShapeDtypeStruct
        heads_shape = (2, split, heavy, depth)
        terms_shape = (units, split, 2, rows, depth)
        held, summed = pl.pallas_call(
            functools.partial(kernel, (pb_size, ka_size, split, group, width)),
            out_shape=[shape(heads_shape, HALF), shape(terms_shape, HALF)],
            in_specs=[in_hbm] * 4,
            out_specs=[in_hbm] * 2,
            scratch_shapes=[
                *[vmem(x.shape, HALF) for x in (keys, values, queries, out_grad)],
                vmem((2, split, rows, depth), HALF),
                vmem((units, 2, span, depth), HALF),
                vmem((units, 2, depth, span), HALF),
                vmem((2, split, heavy, depth), HALF),
                vmem((2, split * heavy, depth), HALF),
                vmem((2, blocks, depth, width), HALF),
                vmem((blocks, units, span, width), F32),
                vmem((blocks, units, span, width), F32),
                vmem((blocks, units, span, width), HALF),
                vmem((units, span, depth), F32),
                vmem((blocks, 8, width), F32),
                vmem((blocks, 8, width), F32),
                vmem((blocks, depth, width), F32),
                vmem((blocks, depth, width), F32),
                vmem((2, split, heavy, depth), HALF),
                vmem((2, units, span, depth), HALF),
                dma((4,)), dma((4,)),
                dma((2, units, split)), dma((2, units, split)), dma((2,)), dma((2,)),
                dma((2, units, split)), dma((2, units, split)), dma((2,)), dma((2,)),
            ],
            compiler_params=pltpu.CompilerParams(
                collective_id=0, has_side_effects=True, vmem_limit_bytes=58 * 2 ** 20),
            name="attention",
        )(keys, values, queries, out_grad)
        results = [shape(x.shape, HALF) for x in (queries, queries, keys, values)]
        return tuple(pl.pallas_call(
            gather_up,
            out_shape=results,
            in_specs=[in_hbm] * 2,
            out_specs=[in_hbm] * 4,
            scratch_shapes=[
                vmem(heads_shape, HALF), vmem(terms_shape, HALF),
                *[vmem(x.shape, HALF) for x in results],
                dma((3,)), dma((4,)),
            ],
            compiler_params=pltpu.CompilerParams(vmem_limit_bytes=58 * 2 ** 20),
            name="gather_up",
        )(held, summed))

    spec = P(("pb", "ka"), "ha", None)
    return jax.shard_map(
        on_device, mesh=mesh, in_specs=(spec,) * 4, out_specs=(spec,) * 4, check_vma=False)
```

time: 26 us -> 24.1 us (0.927)
  Pallas kernels: 25.2 us -> 23.3 us
    pallas_call x1, Pallas kernels: 23 us -> 21 us  [on_device(): pl.pallas_call(functools.partial(kernel, (pb_size, ka_size, split, group,...]
where the time goes in v4:
time: 24.1 us; the launch traced here: 24 us
  Pallas kernels  23.3 us (97%)
  between operations  0.64 us (3%)
    pallas_call x1, Pallas kernels, on_device(): pl.pallas_call(functools.partial(kernel, (pb_size, ka_size, split, group,...  21 us
    pallas_call x1, Pallas kernels, on_device(): pl.pallas_call(gather_up, out_shape=results, in_specs=[in_hbm] * 2, out_s...  2.32 us

profile of v4, /device:TPU:0, one launch (start us, length us, event | category | flops | bytes accessed | tf_op | source)
XLA Modules:
  0.0 24.0 jit_solution(9853799200548437585)
XLA Ops:
  0.6 21.0 %attention.1 = (bf16[2,2,1024,128]{3,2,1,0:T(8,128)(2,1)}, bf16[4,2,2,128,128]{4,3,2,1,0:T(8,128)(2,1)}) custom-call(bf16[128,2,128]{2,1,0:T(2,128)(2,1)} %k_hbm.1, bf16[128,2,128]{2,1,0:T(2,128)(2,1)} %v_hbm.1, bf16[128,16,128]{2,1,0:T(8,128)(2,1)} %q_hbm.1, bf16[128,16,128]{2,1,0:T(8,128)(2,1)} %g_hbm.1), custom_call_target="tpu_custom_call" | custom-call | tf_op jit(solution)/shard_map/attention/pallas_call | solution.py:332
  21.7 2.3 %gather_up.1 = (bf16[128,16,128]{2,1,0:T(8,128)(2,1)}, bf16[128,16,128]{2,1,0:T(8,128)(2,1)}, bf16[128,2,128]{2,1,0:T(2,128)(2,1)}, bf16[128,2,128]{2,1,0:T(2,128)(2,1)}) custom-call(bf16[2,2,1024,128]{3,2,1,0:T(8,128)(2,1)} %get-tuple-element.6.heads_hbm, bf16[4,2,2,128,128]{4,3,2,1,0:T(8,128)(2,1)} %get-tuple-element.7.terms_hbm), custom_call_target="tpu_custom_call" | custom-call | tf_op jit(solution)/shard_map/gather_up/pallas_call | solution.py:364

commit v5 on v4

--- a/solution.py
+++ b/solution.py
@@ -19,7 +19,7 @@
 
 def kernel(dims, k_hbm, v_hbm, q_hbm, g_hbm, heads_out, terms,
            k_ref, v_ref, q_ref, g_ref, kv_stage, kv, kv_t, qg_stage, qg, qg_t,
-           scores, grad_probs, prob_half, sums, tops, dots, out_t, dq_t, back, parts,
+           scores, grad_probs, prob_half, sums, tops, inverses, dots, out_t, dq_t, back, parts,
            load_sem, own_sem, kv_send, kv_recv, qg_send, qg_recv,
            term_send, term_recv, back_send, back_recv):
     pb_size, ka_size, split, group, width = dims
@@ -127,7 +127,7 @@
     for r, e in others:
         pl.semaphore_signal(barrier, inc=1, device_id=device_at(r, e), device_id_type=MESH)
 
-    for which, ref in ((0, k_ref), (1, v_ref)):
+    def push_kv(which, ref):
         loads[which].wait()
         wide = ref[...].astype(F32)
         for h in range(split):
@@ -137,7 +137,8 @@
         for r, e in farthest:
             kv_copy(which, r, e).start()
         kv[0, which, row_slice(core), :] = kv_stage[which, core]
-    for which, ref in ((0, q_ref), (1, g_ref)):
+
+    def push_qg(which, ref):
         loads[2 + which].wait()
         wide = ref[...].astype(F32)
         for h in range(split):
@@ -172,13 +173,13 @@
             weights = jnp.exp2(scores[b, r] * exponent - top)
             scores[b, r] = weights
             total = total + fold_rows(weights, jnp.sum)
-        return 1.0 / jnp.sum(total, axis=0, keepdims=True)
+        inverse = 1.0 / jnp.sum(total, axis=0, keepdims=True)
+        inverses[b] = jnp.broadcast_to(inverse, (8, width))
+        return inverse
 
     def value_terms(b, inverse):
         for r in range(units):
-            probs = scores[b, r] * inverse
-            half = probs.astype(HALF)
-            scores[b, r] = probs
+            half = (scores[b, r] * inverse).astype(HALF)
             prob_half[b, r] = half
             dv = jnp.dot(half, qg[1, block_rows(b), :], preferred_element_type=F32)
             sums[r] = dv if b == 0 else sums[r] + dv
@@ -201,20 +202,23 @@
         if r == 0:
             own_term(which).start()
 
-    def send_heads(which, turned, scale):
-        for half in reversed(range(split)):
-            for b in range(half_blocks):
-                back[which, half, block_rows(b), :] = (
-                    (turned[half * half_blocks + b] * scale).astype(HALF).T)
-            if half:
-                back_copy(which).start()
-            else:
-                own_heads(which).start()
-
+    def send_half(which, half, turned, scale):
+        for b in range(half_blocks):
+            back[which, half, block_rows(b), :] = (
+                (turned[half * half_blocks + b] * scale).astype(HALF).T)
+        if half:
+            back_copy(which).start()
+        else:
+            own_heads(which).start()
+
+    push_kv(0, k_ref)
+    push_qg(0, q_ref)
     for b in range(half_blocks):
         turn_block(0, b)
     arrive(0, 0)
     score(0, 0, half_blocks)
+    push_kv(1, v_ref)
+    push_qg(1, g_ref)
     for b in range(half_blocks):
         turn_block(1, b)
     turn(0, 0)
@@ -245,19 +249,24 @@
         for b in range(blocks):
             grade(r, b)
     for b in range(blocks):
-        dots[b] = jnp.broadcast_to(jnp.sum(dots[b], axis=0, keepdims=True), (8, width))
+        dots[b] = jnp.broadcast_to(
+            jnp.sum(dots[b], axis=0, keepdims=True) * inverses[b, 0:1], (8, width))
     for r in order:
         dk = jnp.zeros((rows * split, depth), F32)
-        for b in range(blocks):
-            grad_scores = (scores[b, r] * (grad_probs[b, r] - dots[b, 0:1])).astype(HALF)
+        for b in reversed(range(blocks)):
+            probs = scores[b, r] * inverses[b, 0:1]
+            grad_scores = (probs * (grad_probs[b, r] - dots[b, 0:1])).astype(HALF)
             dk = dk + jnp.dot(grad_scores, qg[0, block_rows(b), :], preferred_element_type=F32)
             d = jnp.dot(kv_t[r, 0], grad_scores, preferred_element_type=F32)
             dq_t[b] = d if r == order[0] else dq_t[b] + d
+            if r == order[-1] and b == half_blocks and split > 1:
+                send_half(1, 1, dq_t, scaling)
         parts[0, r] = (dk * scaling).astype(HALF)
         send_terms(0, r)
         if r == order[0]:
-            send_heads(0, out_t, 1.0)
-    send_heads(1, dq_t, scaling)
+            for half in reversed(range(split)):
+                send_half(0, half, out_t, 1.0)
+    send_half(1, 0, dq_t, scaling)
 
     for which in range(2):
         own_term(which).wait()
@@ -348,6 +357,7 @@
                 vmem((units, span, depth), F32),
                 vmem((blocks, 8, width), F32),
                 vmem((blocks, 8, width), F32),
+                vmem((blocks, 8, width), F32),
                 vmem((blocks, depth, width), F32),
                 vmem((blocks, depth, width), F32),
                 vmem((2, split, heavy, depth), HALF),

time: 24.1 us -> 24.6 us (1.021)
  Pallas kernels: 23.3 us -> 23.8 us
    pallas_call x1, Pallas kernels: 21 us -> 21.5 us  [on_device(): pl.pallas_call(functools.partial(kernel, (pb_size, ka_size, split, group,...]
where the time goes in v5:
time: 24.6 us; the launch traced here: 24.4 us
  Pallas kernels  23.8 us (97%)
  between operations  0.64 us (3%)
    pallas_call x1, Pallas kernels, on_device(): pl.pallas_call(functools.partial(kernel, (pb_size, ka_size, split, group,...  21.5 us
    pallas_call x1, Pallas kernels, on_device(): pl.pallas_call(gather_up, out_shape=results, in_specs=[in_hbm] * 2, out_s...  2.32 us

profile of v5, /device:TPU:0, one launch (start us, length us, event | category | flops | bytes accessed | tf_op | source)
XLA Modules:
  0.0 24.4 jit_solution(14079433082509404815)
XLA Ops:
  0.6 21.5 %attention.1 = (bf16[2,2,1024,128]{3,2,1,0:T(8,128)(2,1)}, bf16[4,2,2,128,128]{4,3,2,1,0:T(8,128)(2,1)}) custom-call(bf16[128,2,128]{2,1,0:T(2,128)(2,1)} %k_hbm.1, bf16[128,2,128]{2,1,0:T(2,128)(2,1)} %v_hbm.1, bf16[128,16,128]{2,1,0:T(8,128)(2,1)} %q_hbm.1, bf16[128,16,128]{2,1,0:T(8,128)(2,1)} %g_hbm.1), custom_call_target="tpu_custom_call" | custom-call | tf_op jit(solution)/shard_map/attention/pallas_call | solution.py:341
  22.1 2.3 %gather_up.1 = (bf16[128,16,128]{2,1,0:T(8,128)(2,1)}, bf16[128,16,128]{2,1,0:T(8,128)(2,1)}, bf16[128,2,128]{2,1,0:T(2,128)(2,1)}, bf16[128,2,128]{2,1,0:T(2,128)(2,1)}) custom-call(bf16[2,2,1024,128]{3,2,1,0:T(8,128)(2,1)} %get-tuple-element.6.heads_hbm, bf16[4,2,2,128,128]{4,3,2,1,0:T(8,128)(2,1)} %get-tuple-element.7.terms_hbm), custom_call_target="tpu_custom_call" | custom-call | tf_op jit(solution)/shard_map/gather_up/pallas_call | solution.py:374

commit v6 on v5

--- a/solution.py
+++ b/solution.py
@@ -19,7 +19,7 @@
 
 def kernel(dims, k_hbm, v_hbm, q_hbm, g_hbm, heads_out, terms,
            k_ref, v_ref, q_ref, g_ref, kv_stage, kv, kv_t, qg_stage, qg, qg_t,
-           scores, grad_probs, prob_half, sums, tops, inverses, dots, out_t, dq_t, back, parts,
+           scores, grad_probs, prob_half, sums, tops, dots, out_t, dq_t, back, parts,
            load_sem, own_sem, kv_send, kv_recv, qg_send, qg_recv,
            term_send, term_recv, back_send, back_recv):
     pb_size, ka_size, split, group, width = dims
@@ -32,6 +32,7 @@
     heavy = rows * group
     blocks = split * heavy // width
     half_blocks = heavy // width
+    span = rows * split
 
     pb, ka, ha = lax.axis_index("pb"), lax.axis_index("ka"), lax.axis_index("ha")
     core = lax.rem(ka, split)
@@ -62,7 +63,7 @@
     def kv_copy(which, r, e):
         return pltpu.make_async_remote_copy(
             src_ref=kv_stage.at[which, core_at(e)],
-            dst_ref=kv.at[mirror(r), which, row_slice(core), :],
+            dst_ref=kv.at[which, mirror(r), row_slice(core), :],
             send_sem=kv_send.at[which, r, e],
             recv_sem=kv_recv.at[which, mirror(r), (split - e) % split],
             device_id=device_at(r, e), device_id_type=MESH)
@@ -70,7 +71,7 @@
     def kv_arrival(which, r, e):
         return pltpu.make_async_remote_copy(
             src_ref=kv_stage.at[which, core],
-            dst_ref=kv.at[r, which, row_slice(core_at(e)), :],
+            dst_ref=kv.at[which, r, row_slice(core_at(e)), :],
             send_sem=kv_send.at[which, r, e], recv_sem=kv_recv.at[which, r, e],
             device_id=device_at(r, e), device_id_type=MESH)
 
@@ -127,7 +128,7 @@
     for r, e in others:
         pl.semaphore_signal(barrier, inc=1, device_id=device_at(r, e), device_id_type=MESH)
 
-    def push_kv(which, ref):
+    for which, ref in ((0, k_ref), (1, v_ref)):
         loads[which].wait()
         wide = ref[...].astype(F32)
         for h in range(split):
@@ -136,9 +137,8 @@
             pl.semaphore_wait(barrier, len(others))
         for r, e in farthest:
             kv_copy(which, r, e).start()
-        kv[0, which, row_slice(core), :] = kv_stage[which, core]
-
-    def push_qg(which, ref):
+        kv[which, 0, row_slice(core), :] = kv_stage[which, core]
+    for which, ref in ((0, q_ref), (1, g_ref)):
         loads[2 + which].wait()
         wide = ref[...].astype(F32)
         for h in range(split):
@@ -161,7 +161,7 @@
 
     def score(r, first, last):
         for b in range(first, last):
-            s = jnp.dot(kv[r, 0], qg_t[0, b], preferred_element_type=F32)
+            s = jnp.dot(kv[0, r], qg_t[0, b], preferred_element_type=F32)
             scores[b, r] = s
             top = fold_rows(s, jnp.max)
             tops[b] = top if r == 0 else jnp.maximum(tops[b], top)
@@ -173,27 +173,29 @@
             weights = jnp.exp2(scores[b, r] * exponent - top)
             scores[b, r] = weights
             total = total + fold_rows(weights, jnp.sum)
-        inverse = 1.0 / jnp.sum(total, axis=0, keepdims=True)
-        inverses[b] = jnp.broadcast_to(inverse, (8, width))
-        return inverse
+        return 1.0 / jnp.sum(total, axis=0, keepdims=True)
 
     def value_terms(b, inverse):
         for r in range(units):
-            half = (scores[b, r] * inverse).astype(HALF)
-            prob_half[b, r] = half
-            dv = jnp.dot(half, qg[1, block_rows(b), :], preferred_element_type=F32)
-            sums[r] = dv if b == 0 else sums[r] + dv
-
-    def grade(r, b):
-        grad = jnp.dot(kv[r, 1], qg_t[1, b], preferred_element_type=F32)
-        grad_probs[b, r] = grad
-        dot = fold_rows(scores[b, r] * grad, jnp.sum)
-        dots[b] = dot if r == 0 else dots[b] + dot
-        out = jnp.dot(kv_t[r, 1], prob_half[b, r], preferred_element_type=F32)
-        out_t[b] = out if r == 0 else out_t[b] + out
+            probs = scores[b, r] * inverse
+            scores[b, r] = probs
+            prob_half[b, pl.ds(r * span, span), :] = probs.astype(HALF)
+        dv = jnp.dot(prob_half[b], qg[1, block_rows(b), :], preferred_element_type=F32)
+        sums[...] = dv if b == 0 else sums[...] + dv
+
+    def grade(b):
+        values = kv[1].reshape(units * span, depth)
+        grad = jnp.dot(values, qg_t[1, b], preferred_element_type=F32)
+        dot = jnp.zeros((8, width), F32)
+        for r in range(units):
+            part = grad[r * span:(r + 1) * span]
+            grad_probs[b, r] = part
+            dot = dot + fold_rows(scores[b, r] * part, jnp.sum)
+        dots[b] = jnp.broadcast_to(jnp.sum(dot, axis=0, keepdims=True), (8, width))
+        out_t[b] = jnp.dot(kv_t[1], prob_half[b], preferred_element_type=F32)
 
     def turn(which, r):
-        kv_t[r, which] = kv[r, which].T
+        kv_t[which, :, pl.ds(r * span, span)] = kv[which, r].T
 
     def send_terms(which, r):
         for e in range(split):
@@ -211,14 +213,10 @@
         else:
             own_heads(which).start()
 
-    push_kv(0, k_ref)
-    push_qg(0, q_ref)
     for b in range(half_blocks):
         turn_block(0, b)
     arrive(0, 0)
     score(0, 0, half_blocks)
-    push_kv(1, v_ref)
-    push_qg(1, g_ref)
     for b in range(half_blocks):
         turn_block(1, b)
     turn(0, 0)
@@ -234,36 +232,42 @@
         arrive(0, r)
         score(r, 0, blocks)
         turn(0, r)
-    arrive(1, 0)
-    turn(1, 0)
-    for b in range(blocks):
+    order = sorted(range(units), key=far, reverse=True)
+
+    def take_values(b):
         value_terms(b, weigh(b))
-        grade(0, b)
-    order = sorted(range(units), key=far, reverse=True)
-    for r in order:
-        parts[1, r] = sums[r].astype(HALF)
-        send_terms(1, r)
-    for r in range(1, units):
+        if b == blocks - 1:
+            for r in order:
+                parts[1, r] = sums[r * span:(r + 1) * span].astype(HALF)
+                send_terms(1, r)
+
+    ahead = (blocks + 1) // 2
+    for b in range(ahead):
+        take_values(b)
+    for r in range(units):
         arrive(1, r)
         turn(1, r)
-        for b in range(blocks):
-            grade(r, b)
     for b in range(blocks):
-        dots[b] = jnp.broadcast_to(
-            jnp.sum(dots[b], axis=0, keepdims=True) * inverses[b, 0:1], (8, width))
-    for r in order:
-        dk = jnp.zeros((rows * split, depth), F32)
+        if b + ahead < blocks:
+            take_values(b + ahead)
+        grade(b)
+    for first in range(0, units, 2):
+        pair = order[first:first + 2]
+        dk = jnp.zeros((span * len(pair), depth), F32)
+        keys_t = jnp.concatenate([kv_t[0, :, r * span:(r + 1) * span] for r in pair], axis=1)
         for b in reversed(range(blocks)):
-            probs = scores[b, r] * inverses[b, 0:1]
-            grad_scores = (probs * (grad_probs[b, r] - dots[b, 0:1])).astype(HALF)
+            grad_scores = jnp.concatenate([
+                (scores[b, r] * (grad_probs[b, r] - dots[b, 0:1])).astype(HALF) for r in pair
+            ], axis=0)
             dk = dk + jnp.dot(grad_scores, qg[0, block_rows(b), :], preferred_element_type=F32)
-            d = jnp.dot(kv_t[r, 0], grad_scores, preferred_element_type=F32)
-            dq_t[b] = d if r == order[0] else dq_t[b] + d
-            if r == order[-1] and b == half_blocks and split > 1:
+            d = jnp.dot(keys_t, grad_scores, preferred_element_type=F32)
+            dq_t[b] = d if first == 0 else dq_t[b] + d
+            if first + 2 >= units and b == half_blocks and split > 1:
                 send_half(1, 1, dq_t, scaling)
-        parts[0, r] = (dk * scaling).astype(HALF)
-        send_terms(0, r)
-        if r == order[0]:
+        for i, r in enumerate(pair):
+            parts[0, r] = (dk[i * span:(i + 1) * span] * scaling).astype(HALF)
+            send_terms(0, r)
+        if first == 0:
             for half in reversed(range(split)):
                 send_half(0, half, out_t, 1.0)
     send_half(1, 0, dq_t, scaling)
@@ -346,16 +350,15 @@
             scratch_shapes=[
                 *[vmem(x.shape, HALF) for x in (keys, values, queries, out_grad)],
                 vmem((2, split, rows, depth), HALF),
-                vmem((units, 2, span, depth), HALF),
-                vmem((units, 2, depth, span), HALF),
+                vmem((2, units, span, depth), HALF),
+                vmem((2, depth, units * span), HALF),
                 vmem((2, split, heavy, depth), HALF),
                 vmem((2, split * heavy, depth), HALF),
                 vmem((2, blocks, depth, width), HALF),
                 vmem((blocks, units, span, width), F32),
                 vmem((blocks, units, span, width), F32),
-                vmem((blocks, units, span, width), HALF),
-                vmem((units, span, depth), F32),
-                vmem((blocks, 8, width), F32),
+                vmem((blocks, units * span, width), HALF),
+                vmem((units * span, depth), F32),
                 vmem((blocks, 8, width), F32),
                 vmem((blocks, 8, width), F32),
                 vmem((blocks, depth, width), F32),

time: 24.6 us -> 26.6 us (1.081)
  Pallas kernels: 23.8 us -> 25.8 us
    pallas_call x1, Pallas kernels: 21.5 us -> 23.5 us  [on_device(): pl.pallas_call(functools.partial(kernel, (pb_size, ka_size, split, group,...]
where the time goes in v6:
time: 26.6 us; the launch traced here: 26.4 us
  Pallas kernels  25.8 us (97%)
  between operations  0.64 us (2%)
    pallas_call x1, Pallas kernels, on_device(): pl.pallas_call(functools.partial(kernel, (pb_size, ka_size, split, group,...  23.5 us
    pallas_call x1, Pallas kernels, on_device(): pl.pallas_call(gather_up, out_shape=results, in_specs=[in_hbm] * 2, out_s...  2.32 us

profile of v6, /device:TPU:0, one launch (start us, length us, event | category | flops | bytes accessed | tf_op | source)
XLA Modules:
  0.0 26.4 jit_solution(12427525961704371740)
XLA Ops:
  0.6 23.5 %attention.1 = (bf16[2,2,1024,128]{3,2,1,0:T(8,128)(2,1)}, bf16[4,2,2,128,128]{4,3,2,1,0:T(8,128)(2,1)}) custom-call(bf16[128,2,128]{2,1,0:T(2,128)(2,1)} %k_hbm.1, bf16[128,2,128]{2,1,0:T(2,128)(2,1)} %v_hbm.1, bf16[128,16,128]{2,1,0:T(8,128)(2,1)} %q_hbm.1, bf16[128,16,128]{2,1,0:T(8,128)(2,1)} %g_hbm.1), custom_call_target="tpu_custom_call" | custom-call | tf_op jit(solution)/shard_map/attention/pallas_call | solution.py:345
  24.1 2.3 %gather_up.1 = (bf16[128,16,128]{2,1,0:T(8,128)(2,1)}, bf16[128,16,128]{2,1,0:T(8,128)(2,1)}, bf16[128,2,128]{2,1,0:T(2,128)(2,1)}, bf16[128,2,128]{2,1,0:T(2,128)(2,1)}) custom-call(bf16[2,2,1024,128]{3,2,1,0:T(8,128)(2,1)} %get-tuple-element.6.heads_hbm, bf16[4,2,2,128,128]{4,3,2,1,0:T(8,128)(2,1)} %get-tuple-element.7.terms_hbm), custom_call_target="tpu_custom_call" | custom-call | tf_op jit(solution)/shard_map/gather_up/pallas_call | solution.py:377

commit v7 on v4

--- a/solution.py
+++ b/solution.py
@@ -321,7 +321,7 @@
         group = heads // split
         units = pb_size * ka_size // split
         heavy = rows * group
-        width = math.gcd(heavy, 512)
+        width = math.gcd(heavy, 256)
         blocks = split * heavy // width
         span = rows * split
         dma, vmem = pltpu.SemaphoreType.DMA, pltpu.VMEM

time: 24.1 us -> 24.3 us (level)
  no operation moved by 1% of the time
where the time goes in v7:
time: 24.3 us; the launch traced here: 24.1 us
  Pallas kernels  23.5 us (97%)
  between operations  0.64 us (3%)
    pallas_call x1, Pallas kernels, on_device(): pl.pallas_call(functools.partial(kernel, (pb_size, ka_size, split, group,...  21.1 us
    pallas_call x1, Pallas kernels, on_device(): pl.pallas_call(gather_up, out_shape=results, in_specs=[in_hbm] * 2, out_s...  2.32 us

profile of v7, /device:TPU:0, one launch (start us, length us, event | category | flops | bytes accessed | tf_op | source)
XLA Modules:
  0.0 24.1 jit_solution(17649657907338436)
XLA Ops:
  0.6 21.1 %attention.1 = (bf16[2,2,1024,128]{3,2,1,0:T(8,128)(2,1)}, bf16[4,2,2,128,128]{4,3,2,1,0:T(8,128)(2,1)}) custom-call(bf16[128,2,128]{2,1,0:T(2,128)(2,1)} %k_hbm.1, bf16[128,2,128]{2,1,0:T(2,128)(2,1)} %v_hbm.1, bf16[128,16,128]{2,1,0:T(8,128)(2,1)} %q_hbm.1, bf16[128,16,128]{2,1,0:T(8,128)(2,1)} %g_hbm.1), custom_call_target="tpu_custom_call" | custom-call | tf_op jit(solution)/shard_map/attention/pallas_call | solution.py:332
  21.8 2.3 %gather_up.1 = (bf16[128,16,128]{2,1,0:T(8,128)(2,1)}, bf16[128,16,128]{2,1,0:T(8,128)(2,1)}, bf16[128,2,128]{2,1,0:T(2,128)(2,1)}, bf16[128,2,128]{2,1,0:T(2,128)(2,1)}) custom-call(bf16[2,2,1024,128]{3,2,1,0:T(8,128)(2,1)} %get-tuple-element.6.heads_hbm, bf16[4,2,2,128,128]{4,3,2,1,0:T(8,128)(2,1)} %get-tuple-element.7.terms_hbm), custom_call_target="tpu_custom_call" | custom-call | tf_op jit(solution)/shard_map/gather_up/pallas_call | solution.py:364
